TPU v7x, 512 devices: a whole 4x4x16 slice. The times are simulated.
512 devices in a mesh: lat: 16 (over y, x_lo, core), lon: 32 (over x_hi, z).
Axes of the slice: x: 4 (x_hi: 2, x_lo: 2; x = x_hi * 2 + x_lo), y: 4, z: 16, core: 2. Of those that a mesh axis runs over, the one named last changes fastest.
Arguments:
- height: float32 [1, 1536, 12288], P(None, 'lat', 'lon'), may hold values from -6 to 6
- east_wind: float32 [1, 1536, 12288], P(None, 'lat', 'lon'), may hold values from -6 to 6
- north_wind: float32 [1, 1536, 12288], P(None, 'lat', 'lon'), may hold values from -6 to 6
- wave_speed_sq: float32 [1], replicated, may hold values from 0.25 to 1
Outputs:
- height_new: float32 [1, 1536, 12288], P(None, 'lat', 'lon')
- east_new: float32 [1, 1536, 12288], P(None, 'lat', 'lon')
- north_new: float32 [1, 1536, 12288], P(None, 'lat', 'lon')
All inputs are finite; a program needn't handle non-finite values.
Results may differ from a plain program's by a relative error of at most 0.0003.
Values sent between devices are 32-bit elements; how exact they have to be, the bound alone decides.
A program may use at most 64 MiB of HBM per device.

v0:
```python
import math

import jax
import jax.numpy as jnp
from jax import lax
from jax.sharding import PartitionSpec as P

NLON = 12288
INNER = 128
OUTER = 96
SUBSTEPS = 2


COURANT = 0.45
SPIN = 0.3


def extended(shard, sides, width, wrap):
    for axis, dim in sides:
        size, length = (lax.axis_size(axis), shard.shape[dim])
        up = [(i, (i + 1) % size) for i in range(size if wrap else size - 1)]
        down = [(j, i) for i, j in up]
        last = lax.slice_in_dim(shard, length - width, length, axis=dim)
        first = lax.slice_in_dim(shard, 0, width, axis=dim)
        before = lax.ppermute(last, axis, up)
        after = lax.ppermute(first, axis, down)
        shard = jnp.concatenate([before, shard, after], axis=dim)
    return shard


def latitudes(global_rows, nlat_total):
    return -0.5 * math.pi + (global_rows.astype(jnp.float32) + 0.5) * (math.pi / nlat_total)


def circle(first, second, period):
    product = (
        jnp.arange(first, dtype=jnp.int32)[:, None]
        * jnp.arange(second, dtype=jnp.int32)[None, :]
        % period
    )
    angle = product.astype(jnp.float32) * (2.0 * math.pi / period)
    return (jnp.cos(angle), jnp.sin(angle))


def polar_filter(rows_full, cosine):
    row_count = rows_full.shape[0]
    highest = lax.Precision.HIGHEST
    grid = rows_full.reshape(row_count, OUTER, INNER)
    outer_cos, outer_sin = circle(OUTER, OUTER, OUTER)
    inner_cos, inner_sin = circle(INNER, INNER, INNER)
    twist_cos, twist_sin = circle(OUTER, INNER, NLON)
    first_real = jnp.einsum("qan,ak->qkn", grid, outer_cos, precision=highest)
    first_imag = -jnp.einsum("qan,ak->qkn", grid, outer_sin, precision=highest)
    turned_real = first_real * twist_cos + first_imag * twist_sin
    turned_imag = first_imag * twist_cos - first_real * twist_sin
    spec_real = jnp.einsum("qkn,nm->qkm", turned_real, inner_cos, precision=highest) + jnp.einsum(
        "qkn,nm->qkm", turned_imag, inner_sin, precision=highest
    )
    spec_imag = jnp.einsum("qkn,nm->qkm", turned_imag, inner_cos, precision=highest) - jnp.einsum(
        "qkn,nm->qkm", turned_real, inner_sin, precision=highest
    )
    wave = (
        jnp.arange(OUTER, dtype=jnp.int32)[:, None]
        + OUTER * jnp.arange(INNER, dtype=jnp.int32)[None, :]
    )
    half_sine = 0.5 * jnp.abs(jnp.sin(wave.astype(jnp.float32) * (math.pi / NLON)))
    column = cosine[:, None, None]
    factor = column / jnp.maximum(half_sine[None], column)
    spec_real = spec_real * factor
    spec_imag = spec_imag * factor
    back_real = jnp.einsum("qkm,mn->qkn", spec_real, inner_cos, precision=highest) - jnp.einsum(
        "qkm,mn->qkn", spec_imag, inner_sin, precision=highest
    )
    back_imag = jnp.einsum("qkm,mn->qkn", spec_imag, inner_cos, precision=highest) + jnp.einsum(
        "qkm,mn->qkn", spec_real, inner_sin, precision=highest
    )
    spun_real = back_real * twist_cos - back_imag * twist_sin
    spun_imag = back_imag * twist_cos + back_real * twist_sin
    result = jnp.einsum("qkn,ka->qan", spun_real, outer_cos, precision=highest) - jnp.einsum(
        "qkn,ka->qan", spun_imag, outer_sin, precision=highest
    )
    return (result / NLON).reshape(row_count, NLON)


def keep_rows(rows_full, cosine):
    return rows_full


def along_rows(flat_rows, anchor, nlat_total, needed):
    groups = lax.axis_size("lon")
    total, cells = flat_rows.shape
    share = total // groups
    sent = lax.all_to_all(
        flat_rows.reshape(groups, share, cells), "lon", split_axis=0, concat_axis=2, tiled=True
    )
    mine = lax.dynamic_slice_in_dim(anchor, lax.axis_index("lon") * share, share)
    cosine = jnp.cos(latitudes(mine, nlat_total))
    filtered = lax.cond(needed, polar_filter, keep_rows, sent[0], cosine)
    returned = lax.all_to_all(filtered[None], "lon", split_axis=2, concat_axis=0, tiled=True)
    return returned.reshape(total, cells)


def smooth(increment, band, nlat_total):
    fields, rows, cells = increment.shape
    anchor = band * rows + jnp.arange(rows, dtype=jnp.int32)
    sixth = nlat_total // 6
    needed = jnp.logical_or(band * rows < sixth, (band + 1) * rows > nlat_total - sixth)
    treated = along_rows(
        increment.reshape(fields * rows, cells), jnp.tile(anchor, fields), nlat_total, needed
    )
    return treated.reshape(fields, rows, cells)


def body(height, east_wind, north_wind, wave_speed_sq):
    layers, rows, cells = height.shape
    nlat_total = rows * lax.axis_size("lat")
    band = lax.axis_index("lat")
    latitude = latitudes(band * rows + jnp.arange(rows, dtype=jnp.int32), nlat_total)
    col_cos = jnp.cos(latitude)[None, :, None]
    col_sin = jnp.sin(latitude)[None, :, None]
    north_scale = COURANT * 2.0 * nlat_total / NLON
    speed = wave_speed_sq[:, None, None]
    thick, east, north = (height, east_wind, north_wind)
    for step in range(SUBSTEPS):
        wide = extended(thick, (("lon", 2),), 1, True)
        tall = extended(thick, (("lat", 1),), 1, False)
        east_grad = (wide[:, :, 2:] - wide[:, :, :-2]) * 0.5
        north_grad = (tall[:, 2:] - tall[:, :-2]) * 0.5
        east_inc = -(COURANT / col_cos) * east_grad + SPIN * col_sin * north
        north_inc = -north_scale * north_grad - SPIN * col_sin * east
        both = smooth(jnp.concatenate([east_inc, north_inc], axis=0), band, nlat_total)
        east = east + both[:layers]
        north = north + both[layers:]
        east_wide = extended(east, (("lon", 2),), 1, True)
        flux_tall = extended(north * col_cos, (("lat", 1),), 1, False)
        spread = COURANT / col_cos * (
            (east_wide[:, :, 2:] - east_wide[:, :, :-2]) * 0.5
        ) + north_scale / col_cos * ((flux_tall[:, 2:] - flux_tall[:, :-2]) * 0.5)
        thick = thick + smooth(-speed * spread, band, nlat_total)
    return (thick, east, north)


def solution(mesh):
    in_specs = (P(None, "lat", "lon"), P(None, "lat", "lon"), P(None, "lat", "lon"), P())
    out_specs = (P(None, "lat", "lon"), P(None, "lat", "lon"), P(None, "lat", "lon"))
    return jax.shard_map(body, mesh=mesh, in_specs=in_specs, out_specs=out_specs, check_vma=False)
```

profile of v0, /device:TPU:1, one launch (start us, length us, event | category | flops | bytes accessed | tf_op | source)
XLA Modules:
  0.0 661.5 jit_solution(16227098313169869724)
XLA Ops:
  1.4 8.8 %collective-permute-start.2 = (f32[1,1,384]{2,1,0:T(1,128)S(1)}, f32[1,1,384]{2,1,0:T(1,128)S(1)}, u32[]{:S(2)}, u32[]{:S(2)}) collective-permute-start(f32[1,1,384]{2,1,0:T(1,128)S(1)} %get-tuple-element.121), channel_id=1, source_target_pairs={{32,0},{64,32},{96,64},{128,96},{160,128},{192,160},{224,192},{256... | collective-permute-start | bytes 4616 | tf_op jit(solution)/shard_map/ppermute | solution.py:26
  13.0 9.3 %collective-permute-start = (f32[1,96,1]{2,1,0:T(8,128)S(1)}, f32[1,96,1]{2,1,0:T(8,128)S(1)}, u32[]{:S(2)}, u32[]{:S(2)}) collective-permute-start(f32[1,96,1]{2,1,0:T(8,128)S(1)} %get-tuple-element.119), channel_id=1, source_target_pairs={{1,0},{2,1},{3,2},{4,3},{5,4},{6,5},{7,6},{8,7},{9,8},{10,9},{11,1... | collective-permute-start | bytes 1160 | tf_op jit(solution)/shard_map/ppermute | solution.py:26
  24.2 7.1 %collective-permute-done.1 = f32[1,96,1]{2,1,0:T(8,128)S(1)} collective-permute-done((f32[1,96,1]{2,1,0:T(8,128)S(1)}, f32[1,96,1]{2,1,0:T(8,128)S(1)}, u32[]{:S(2)}, u32[]{:S(2)}) %collective-permute-start.1) | collective-permute-done | bytes 416 | tf_op jit(solution)/shard_map/ppermute | solution.py:25
  37.8 27.1 %all-to-all-done = f32[32,6,384]{2,1,0:T(8,128)S(1)} async-done(((f32[32,6,384]{2,1,0:T(8,128)}), f32[32,6,384]{2,1,0:T(8,128)S(1)}, u32[]{:S(2)}, u32[]{:S(2)}) %all-to-all-start) | async-done | bytes 294944 | tf_op jit(solution)/shard_map/all_to_all | solution.py:93
  64.9 9.0 %conditional.4 = (f32[6,12288]{1,0:T(8,128)S(1)}) conditional(s32[]{:T(128)} %convert_element_type.261, (f32[1,6,32,384]{3,1,2,0:T(8,128)S(1)}) %tuple.94, (f32[1,6,32,384]{3,1,2,0:T(8,128)S(1)}, f32[6]{0:T(128)S(1)}) %tuple.95), branch_computations={%region_0.0_spmd, %region_1.2_spmd} | conditional | flops 1250332800 | bytes 12928056 | solution.py:98
  78.5 56.4 %reduce = f32[12288,6]{1,0:T(8,128)} reduce(f32[12288,1,6]{2,1,0:T(1,128)} %bitcast.251, f32[]{:T(128)} %broadcast.908), dimensions={1}, to_apply=%bitcast.215.reduce_sub_computation | reduce | bytes 589828
  134.9 7.5 %reshape.342 = f32[32,1,2304]{2,1,0:T(1,128)} reshape(f32[12288,6]{1,0:T(8,128)} %reduce) | data formatting | bytes 589824
  147.4 22.4 %all-to-all-done.1 = f32[32,1,2304]{2,1,0:T(1,128)S(1)} async-done(((f32[32,1,2304]{2,1,0:T(1,128)}), f32[32,1,2304]{2,1,0:T(1,128)S(1)}, u32[]{:S(2)}, u32[]{:S(2)}) %all-to-all-start.1) | async-done | bytes 294944 | tf_op jit(solution)/shard_map/all_to_all | solution.py:99
  171.2 11.0 %reshape.343 = f32[12288,1,6]{2,1,0:T(1,128)} reshape(f32[32,2304]{1,0:T(8,128)S(1)} %reduce.1) | data formatting | bytes 589824
  207.6 19.4 %all-to-all-done.2 = f32[32,3,384]{2,1,0:T(4,128)S(1)} async-done(((f32[32,3,384]{2,1,0:T(4,128)}), f32[32,3,384]{2,1,0:T(4,128)S(1)}, u32[]{:S(2)}, u32[]{:S(2)}) %all-to-all-start.2) | async-done | bytes 147488 | tf_op jit(solution)/shard_map/all_to_all | solution.py:93
  227.0 7.2 %conditional.5 = (f32[3,12288]{1,0:T(4,128)S(1)}) conditional(s32[]{:T(128)} %convert_element_type.261, (f32[1,3,32,384]{3,1,2,0:T(4,128)S(1)}) %tuple.98, (f32[1,3,32,384]{3,1,2,0:T(4,128)S(1)}, f32[3]{0:T(128)S(1)}) %tuple.99), branch_computations={%region_2.3_spmd, %region_3.4_spmd} | conditional | flops 626335872 | bytes 6882336 | solution.py:98
  238.3 56.4 %reduce.2 = f32[12288,3]{1,0:T(8,128)} reduce(f32[12288,1,3]{2,1,0:T(1,128)} %bitcast.253, f32[]{:T(128)} %broadcast.908), dimensions={1}, to_apply=%bitcast.217.reduce_sub_computation | reduce | bytes 294916
  300.9 21.1 %all_to_all.128 = f32[32,1,1152]{2,1,0:T(1,128)S(1)} all-to-all(f32[32,1,1152]{2,1,0:T(1,128)S(1)} %reshape.344), channel_id=1, replica_groups=mesh['lat'=16,'lon'=32] {'lon'}, dimensions={0} | all-to-all | bytes 294912 | tf_op jit(solution)/shard_map/all_to_all | solution.py:99
  322.9 11.0 %reshape.345 = f32[12288,1,3]{2,1,0:T(1,128)} reshape(f32[32,1152]{1,0:T(8,128)S(1)} %reduce.3) | data formatting | bytes 294912
  356.4 28.9 %all_to_all.129 = f32[32,6,384]{2,1,0:T(8,128)S(1)} all-to-all(f32[32,6,384]{2,1,0:T(8,128)S(1)} %reshape_reshape.23), channel_id=1, replica_groups=mesh['lat'=16,'lon'=32] {'lon'}, dimensions={0} | all-to-all | bytes 589824 | tf_op jit(solution)/shard_map/all_to_all | solution.py:93
  385.3 9.1 %conditional.6 = (f32[6,12288]{1,0:T(8,128)S(1)}) conditional(s32[]{:T(128)} %convert_element_type.261, (f32[1,6,32,384]{3,1,2,0:T(8,128)S(1)}) %tuple.96, (f32[1,6,32,384]{3,1,2,0:T(8,128)S(1)}, f32[6]{0:T(128)S(1)}) %tuple.97), branch_computations={%region_4.5_spmd, %region_5.6_spmd} | conditional | flops 1250332800 | bytes 12928056 | solution.py:98
  398.5 56.4 %reduce.4 = f32[12288,6]{1,0:T(8,128)} reduce(f32[12288,1,6]{2,1,0:T(1,128)} %bitcast.255, f32[]{:T(128)} %broadcast.908), dimensions={1}, to_apply=%bitcast.219.reduce_sub_computation | reduce | bytes 589828
  461.9 28.8 %all_to_all.130 = f32[32,1,2304]{2,1,0:T(1,128)S(1)} all-to-all(f32[32,1,2304]{2,1,0:T(1,128)S(1)} %reshape.346), channel_id=1, replica_groups=mesh['lat'=16,'lon'=32] {'lon'}, dimensions={0} | all-to-all | bytes 589824 | tf_op jit(solution)/shard_map/all_to_all | solution.py:99
  492.0 11.0 %reshape.347 = f32[12288,1,6]{2,1,0:T(1,128)} reshape(f32[32,2304]{1,0:T(8,128)S(1)} %reduce.5) | data formatting | bytes 589824
  527.4 20.9 %all_to_all.131 = f32[32,3,384]{2,1,0:T(4,128)S(1)} all-to-all(f32[32,3,384]{2,1,0:T(4,128)S(1)} %reshape_reshape.24), channel_id=1, replica_groups=mesh['lat'=16,'lon'=32] {'lon'}, dimensions={0} | all-to-all | bytes 294912 | tf_op jit(solution)/shard_map/all_to_all | solution.py:93
  548.3 7.3 %conditional.7 = (f32[3,12288]{1,0:T(4,128)S(1)}) conditional(s32[]{:T(128)} %convert_element_type.261, (f32[1,3,32,384]{3,1,2,0:T(4,128)S(1)}) %tuple.100, (f32[1,3,32,384]{3,1,2,0:T(4,128)S(1)}, f32[3]{0:T(128)S(1)}) %tuple.101), branch_computations={%region_6.7_spmd, %region_7.8_spmd} | conditional | flops 626335872 | bytes 6882336 | solution.py:98
  559.7 56.4 %reduce.6 = f32[12288,3]{1,0:T(8,128)} reduce(f32[12288,1,3]{2,1,0:T(1,128)} %bitcast.257, f32[]{:T(128)} %broadcast.908), dimensions={1}, to_apply=%bitcast.221.reduce_sub_computation | reduce | bytes 294916
  622.3 21.4 %all_to_all.132 = f32[32,1,1152]{2,1,0:T(1,128)S(1)} all-to-all(f32[32,1,1152]{2,1,0:T(1,128)S(1)} %reshape.348), channel_id=1, replica_groups=mesh['lat'=16,'lon'=32] {'lon'}, dimensions={0} | all-to-all | bytes 294912 | tf_op jit(solution)/shard_map/all_to_all | solution.py:99
  644.7 11.0 %reshape.349 = f32[12288,1,3]{2,1,0:T(1,128)} reshape(f32[32,1152]{1,0:T(8,128)S(1)} %reduce.7) | data formatting | bytes 294912
  (168 shorter events, 163.9 us)
Async XLA Ops:
  1.4 30.0 %collective-permute-start.2 = (f32[1,1,384]{2,1,0:T(1,128)S(1)}, f32[1,1,384]{2,1,0:T(1,128)S(1)}, u32[]{:S(2)}, u32[]{:S(2)}) collective-permute-start(f32[1,1,384]{2,1,0:T(1,128)S(1)} %get-tuple-element.121), channel_id=1, source_target_pairs={{32,0},{64,32},{96,64},{128,96},{160,128},{192,160},{224,192},{256... | collective-permute-start | bytes 4616 | tf_op jit(solution)/shard_map/ppermute | solution.py:26
  10.1 21.2 %collective-permute-start.3 = (f32[1,1,384]{2,1,0:T(1,128)S(1)}, f32[1,1,384]{2,1,0:T(1,128)S(1)}, u32[]{:S(2)}, u32[]{:S(2)}) collective-permute-start(f32[1,1,384]{2,1,0:T(1,128)S(1)} %get-tuple-element.122), channel_id=1, source_target_pairs={{0,32},{32,64},{64,96},{96,128},{128,160},{160,192},{192,224},{224... | collective-permute-start | bytes 4616 | tf_op jit(solution)/shard_map/ppermute | solution.py:25
  13.0 11.3 %collective-permute-start = (f32[1,96,1]{2,1,0:T(8,128)S(1)}, f32[1,96,1]{2,1,0:T(8,128)S(1)}, u32[]{:S(2)}, u32[]{:S(2)}) collective-permute-start(f32[1,96,1]{2,1,0:T(8,128)S(1)} %get-tuple-element.119), channel_id=1, source_target_pairs={{1,0},{2,1},{3,2},{4,3},{5,4},{6,5},{7,6},{8,7},{9,8},{10,9},{11,1... | collective-permute-start | bytes 1160 | tf_op jit(solution)/shard_map/ppermute | solution.py:26
  22.2 9.1 %collective-permute-start.1 = (f32[1,96,1]{2,1,0:T(8,128)S(1)}, f32[1,96,1]{2,1,0:T(8,128)S(1)}, u32[]{:S(2)}, u32[]{:S(2)}) collective-permute-start(f32[1,96,1]{2,1,0:T(8,128)S(1)} %get-tuple-element.120), channel_id=1, source_target_pairs={{0,1},{1,2},{2,3},{3,4},{4,5},{5,6},{6,7},{7,8},{8,9},{9,10},{10,1... | collective-permute-start | bytes 1160 | tf_op jit(solution)/shard_map/ppermute | solution.py:25
  33.6 31.2 %all-to-all-start = ((f32[32,6,384]{2,1,0:T(8,128)}), f32[32,6,384]{2,1,0:T(8,128)S(1)}, u32[]{:S(2)}, u32[]{:S(2)}) async-start(f32[32,6,384]{2,1,0:T(8,128)} %reshape_reshape.20), calls=%async_computation | async-start | bytes 786432 | tf_op jit(solution)/shard_map/all_to_all | solution.py:93
  142.4 27.4 %all-to-all-start.1 = ((f32[32,1,2304]{2,1,0:T(1,128)}), f32[32,1,2304]{2,1,0:T(1,128)S(1)}, u32[]{:S(2)}, u32[]{:S(2)}) async-start(f32[32,1,2304]{2,1,0:T(1,128)} %reshape.342), calls=%async_computation.1 | async-start | bytes 589824 | tf_op jit(solution)/shard_map/all_to_all | solution.py:99
  171.2 15.7 %copy-start.3 = (f32[1,96,384]{2,1,0:T(8,128)S(1)}, f32[1,96,384]{2,1,0:T(8,128)}, u32[]{:S(2)}) copy-start(f32[1,96,384]{2,1,0:T(8,128)} %param.13) | copy-start | bytes 442372
  171.2 21.3 %copy-start = (f32[1,96,384]{2,1,0:T(8,128)S(1)}, f32[1,96,384]{2,1,0:T(8,128)}, u32[]{:S(2)}) copy-start(f32[1,96,384]{2,1,0:T(8,128)} %param.14) | copy-start | bytes 442372
  187.0 14.1 %collective-permute-start.4 = (f32[1,96,1]{2,1,0:T(8,128)S(1)}, f32[1,96,1]{2,1,0:T(8,128)S(1)}, u32[]{:S(2)}, u32[]{:S(2)}) collective-permute-start(f32[1,96,1]{2,1,0:T(8,128)S(1)} %get-tuple-element.115), channel_id=1, source_target_pairs={{1,0},{2,1},{3,2},{4,3},{5,4},{6,5},{7,6},{8,7},{9,8},{10,9},{11,1... | collective-permute-start | bytes 1160 | tf_op jit(solution)/shard_map/ppermute | solution.py:26
  189.0 12.2 %collective-permute-start.5 = (f32[1,96,1]{2,1,0:T(8,128)S(1)}, f32[1,96,1]{2,1,0:T(8,128)S(1)}, u32[]{:S(2)}, u32[]{:S(2)}) collective-permute-start(f32[1,96,1]{2,1,0:T(8,128)S(1)} %get-tuple-element.116), channel_id=1, source_target_pairs={{0,1},{1,2},{2,3},{3,4},{4,5},{5,6},{6,7},{7,8},{8,9},{9,10},{10,1... | collective-permute-start | bytes 1160 | tf_op jit(solution)/shard_map/ppermute | solution.py:25
  192.6 8.5 %collective-permute-start.6 = (f32[1,1,384]{2,1,0:T(1,128)S(1)}, f32[1,1,384]{2,1,0:T(1,128)S(1)}, u32[]{:S(2)}, u32[]{:S(2)}) collective-permute-start(f32[1,1,384]{2,1,0:T(1,128)S(1)} %get-tuple-element.117), channel_id=1, source_target_pairs={{32,0},{64,32},{96,64},{128,96},{160,128},{192,160},{224,192},{256... | collective-permute-start | bytes 4616 | tf_op jit(solution)/shard_map/ppermute | solution.py:26
  198.5 3.0 collective-permute-start.7
  202.4 24.6 %all-to-all-start.2 = ((f32[32,3,384]{2,1,0:T(4,128)}), f32[32,3,384]{2,1,0:T(4,128)S(1)}, u32[]{:S(2)}, u32[]{:S(2)}) async-start(f32[32,3,384]{2,1,0:T(4,128)} %reshape_reshape.21), calls=%async_computation.2 | async-start | bytes 393216 | tf_op jit(solution)/shard_map/all_to_all | solution.py:93
  322.9 15.7 %copy-start.1 = (f32[1,96,384]{2,1,0:T(8,128)S(1)}, f32[1,96,384]{2,1,0:T(8,128)}, u32[]{:S(2)}) copy-start(f32[1,96,384]{2,1,0:T(8,128)} %param.12) | copy-start | bytes 442372
  338.6 17.5 %collective-permute-start.10 = (f32[1,1,384]{2,1,0:T(1,128)S(1)}, f32[1,1,384]{2,1,0:T(1,128)S(1)}, u32[]{:S(2)}, u32[]{:S(2)}) collective-permute-start(f32[1,1,384]{2,1,0:T(1,128)S(1)} %get-tuple-element.113), channel_id=1, source_target_pairs={{32,0},{64,32},{96,64},{128,96},{160,128},{192,160},{224,192},{256... | collective-permute-start | bytes 4616 | tf_op jit(solution)/shard_map/ppermute | solution.py:26
  343.7 12.4 %collective-permute-start.11 = (f32[1,1,384]{2,1,0:T(1,128)S(1)}, f32[1,1,384]{2,1,0:T(1,128)S(1)}, u32[]{:S(2)}, u32[]{:S(2)}) collective-permute-start(f32[1,1,384]{2,1,0:T(1,128)S(1)} %get-tuple-element.114), channel_id=1, source_target_pairs={{0,32},{32,64},{64,96},{96,128},{128,160},{160,192},{192,224},{224... | collective-permute-start | bytes 4616 | tf_op jit(solution)/shard_map/ppermute | solution.py:25
  345.7 5.3 collective-permute-start.8
  347.6 8.4 %collective-permute-start.9 = (f32[1,96,1]{2,1,0:T(8,128)S(1)}, f32[1,96,1]{2,1,0:T(8,128)S(1)}, u32[]{:S(2)}, u32[]{:S(2)}) collective-permute-start(f32[1,96,1]{2,1,0:T(8,128)S(1)} %get-tuple-element.112), channel_id=1, source_target_pairs={{0,1},{1,2},{2,3},{3,4},{4,5},{5,6},{6,7},{7,8},{8,9},{9,10},{10,1... | collective-permute-start | bytes 1160 | tf_op jit(solution)/shard_map/ppermute | solution.py:25
  507.7 52.0 %copy-start.2 = (f32[1,96,384]{2,1,0:T(8,128)}, f32[1,96,384]{2,1,0:T(8,128)S(1)}, u32[]{:S(2)}) copy-start(f32[1,96,384]{2,1,0:T(8,128)S(1)} %copy_add_fusion.2) | copy-start | bytes 442372
  508.6 18.6 %collective-permute-start.14 = (f32[1,1,384]{2,1,0:T(1,128)S(1)}, f32[1,1,384]{2,1,0:T(1,128)S(1)}, u32[]{:S(2)}, u32[]{:S(2)}) collective-permute-start(f32[1,1,384]{2,1,0:T(1,128)S(1)} %get-tuple-element.109), channel_id=1, source_target_pairs={{32,0},{64,32},{96,64},{128,96},{160,128},{192,160},{224,192},{256... | collective-permute-start | bytes 4616 | tf_op jit(solution)/shard_map/ppermute | solution.py:26
  514.8 12.4 %collective-permute-start.15 = (f32[1,1,384]{2,1,0:T(1,128)S(1)}, f32[1,1,384]{2,1,0:T(1,128)S(1)}, u32[]{:S(2)}, u32[]{:S(2)}) collective-permute-start(f32[1,1,384]{2,1,0:T(1,128)S(1)} %get-tuple-element.110), channel_id=1, source_target_pairs={{0,32},{32,64},{64,96},{96,128},{128,160},{160,192},{192,224},{224... | collective-permute-start | bytes 4616 | tf_op jit(solution)/shard_map/ppermute | solution.py:25
  516.8 5.3 collective-permute-start.12
  518.7 8.4 %collective-permute-start.13 = (f32[1,96,1]{2,1,0:T(8,128)S(1)}, f32[1,96,1]{2,1,0:T(8,128)S(1)}, u32[]{:S(2)}, u32[]{:S(2)}) collective-permute-start(f32[1,96,1]{2,1,0:T(8,128)S(1)} %get-tuple-element.108), channel_id=1, source_target_pairs={{0,1},{1,2},{2,3},{3,4},{4,5},{5,6},{6,7},{7,8},{8,9},{9,10},{10,1... | collective-permute-start | bytes 1160 | tf_op jit(solution)/shard_map/ppermute | solution.py:25
where the time goes:
time: 671 us; the launch traced here: 662 us
  other arithmetic  236 us (35%)
  blocking collectives  121 us (18%)
  local copies, waits for them, and re-layouts  111 us (17%)
  waiting for transfers between devices  86.6 us (13%)
  starting transfers between devices  74.4 us (11%)
  matrix products  27.6 us (4%)
    unnamed x4, other arithmetic  226 us
    unnamed x17, local copies, waits for them, and re-layouts  71.4 us
    all_to_all x3, blocking collectives, along_rows(): lax.all_to_all(filtered[None], 'lon', split_axis=2, concat_axis=0, tiled=...  71.3 us
    all_to_all x2, blocking collectives, along_rows(): lax.all_to_all(flat_rows.reshape(groups, share, cells), 'lon', split_axis...  49.8 us
    all_to_all x2, waiting for transfers between devices, along_rows(): lax.all_to_all(flat_rows.reshape(groups, share, cells), 'lon', split_axis...  46.5 us
    ppermute x8, starting transfers between devices, extended(): after = lax.ppermute(first, axis, down)  40.9 us
    all_to_all x1, waiting for transfers between devices, along_rows(): lax.all_to_all(filtered[None], 'lon', split_axis=2, concat_axis=0, tiled=...  22.4 us
    ppermute x8, starting transfers between devices, extended(): before = lax.ppermute(last, axis, up)  19.7 us
  transfers between devices with their start and end apart: 19, of which 7 were waited for; matrix products, arithmetic and copies ran while one was open for 0% of the time, Pallas kernels for 0%

commit v1 on v0

v1 whole, which is shorter than its diff:
```python
import math

import jax
import jax.numpy as jnp
import ml_dtypes
import numpy as np
from jax import lax
from jax.experimental import pallas as pl
from jax.experimental.pallas import tpu as pltpu
from jax.sharding import PartitionSpec as P

NLON, NLAT = 12288, 1536
ROWS, CELLS = 96, 384
OUTER, INNER = 96, 128
HALF = 56
COURANT, SPIN = 0.45, 0.3
NORTH = COURANT * 2.0 * NLAT / NLON
FINAL = 260
LAST = 264
MESH = pl.DeviceIdType.MESH
F32, BF16 = jnp.float32, jnp.bfloat16
GROUPS = ((0,), (1, 2))


def split(table):
    high = table.astype(ml_dtypes.bfloat16)
    low = (table - high.astype(np.float64)).astype(ml_dtypes.bfloat16)
    return high, low


def tables():
    a = np.array([3 * d + s for s in range(3) for d in range(32)])
    k1 = np.arange(HALF)
    live = (k1 <= OUTER // 2).astype(np.float64)
    angle = 2 * np.pi * ((k1[:, None] * a[None, :]) % OUTER) / OUTER
    first = np.concatenate([np.cos(angle) * live[:, None], -np.sin(angle) * live[:, None]], axis=0)
    weight = live * np.where((k1 == 0) | (k1 == OUTER // 2), 1.0, 2.0) / NLON
    last = np.concatenate([np.cos(angle) * weight[:, None], -np.sin(angle) * weight[:, None]], axis=0).T
    n = np.arange(INNER)
    turn = 2 * np.pi * (k1[:, None] * n[None, :]) / NLON
    inner = 2 * np.pi * ((n[:, None] * n[None, :]) % INNER) / INNER
    cos, sin = np.cos(inner), np.sin(inner)
    forward = np.block([[cos, -sin], [sin, cos]])
    backward = np.block([[cos, sin], [-sin, cos]])
    wave = k1[:, None] + OUTER * n[None, :]
    steep = np.sin(2 * np.pi * wave / NLON) * live[:, None]
    half_sine = np.where(live[:, None] > 0, 0.5 * np.abs(np.sin(np.pi * wave / NLON)), 1.0)
    first_high, first_low = split(first)
    last_high, last_low = split(last)
    forward_high, forward_low = split(forward)
    backward_high, backward_low = split(backward)
    grid = np.stack([np.cos(turn), np.sin(turn), steep, half_sine]).astype(np.float32)
    row = np.arange(-1, LAST + 1)
    latitude = -0.5 * np.pi + (row + 0.5) * np.pi / NLAT
    ring = np.stack([np.cos(latitude), np.sin(latitude)]).astype(np.float32)
    return (
        np.concatenate([first_high, first_low, first_high], axis=1),
        np.concatenate([last_high, last_low, last_high], axis=1),
        np.stack([forward_high, forward_low]),
        np.stack([backward_high, backward_low]),
        grid,
        ring,
    )


def parts(value):
    high = value.astype(BF16)
    return high, (value - high.astype(F32)).astype(BF16)


def dot(left, right):
    return jnp.dot(left, right, preferred_element_type=F32)


def outer_step(table, value):
    high, low = parts(value)
    return dot(table, jnp.concatenate([high, high, low], axis=0))


def inner_step(table, value):
    high, low = parts(value)
    return dot(high, table[0]) + dot(low, table[0]) + dot(high, table[1])


def kernel(
    h_ref, u_ref, v_ref, speed_ref, ring_ref, first_ref, last_ref, fore_ref, back_ref, grid_ref,
    h_out, u_out, v_out,
    src0, src1, relay0, relay1, recv0, recv1, snd0, snd1, home0, home1, ret0, ret1,
    nb, state, packed, sides, ext,
    send_a, recv_a, send_b, recv_b, send_c, recv_c, send_d, recv_d,
    send_x, recv_x, send_s, recv_s, send_r, recv_r,
):
    fields, outs = (h_ref, u_ref, v_ref), (h_out, u_out, v_out)
    src, relay, recv = (src0, src1), (relay0, relay1), (recv0, recv1)
    snd, home, ret = (snd0, snd1), (home0, home1), (ret0, ret1)
    lat, lon = lax.axis_index("lat"), lax.axis_index("lon")
    south = lat >= 8
    band = jnp.where(south, 15 - lat, lat)
    core = lax.rem(band, 2)
    x_hi, z = lax.div(lon, 16), lax.rem(lon, 16)
    x = 2 * x_hi + lax.rem(lax.div(band, 2), 2)
    line = jnp.where(band < 4, x, 7 - x)
    place = 2 * z + core
    slab = 16 * core + z
    wide = line >= 6
    double = jnp.logical_and(wide, place >= 28)
    count = jnp.where(double, 2, 1)
    chain = 32 * line + place
    line_rows = jnp.where(wide, 36, 32)
    line_row = place + jnp.where(double, place - 28, 0)
    row0 = 32 * line + jnp.where(line == 7, 4, 0) + line_row
    flip = jnp.where(south, -1.0, 1.0).astype(F32)
    source = band <= 2
    stencil = band >= 2

    def member(to_line, to_z, to_core):
        to_x = jnp.where(to_line < 4, to_line, 7 - to_line)
        to_band = 4 * lax.div(to_line, 4) + 2 * lax.rem(to_x, 2) + to_core
        return jnp.where(south, 15 - to_band, to_band), 16 * lax.div(to_x, 2) + to_z

    def send(here, there, send_sem, recv_sem, target):
        same = jnp.logical_and(target[0] == lat, target[1] == lon)

        @pl.when(same)
        def _():
            pltpu.make_async_copy(here, there, recv_sem).start()

        @pl.when(jnp.logical_not(same))
        def _():
            pltpu.make_async_remote_copy(
                src_ref=here, dst_ref=there, send_sem=send_sem, recv_sem=recv_sem, device_id=target, device_id_type=MESH
            ).start()

    def remote(here, there, send_sem, recv_sem, target):
        pltpu.make_async_remote_copy(
            src_ref=here, dst_ref=there, send_sem=send_sem, recv_sem=recv_sem, device_id=target, device_id_type=MESH
        ).start()

    def landed(ref, sem):
        pltpu.make_async_copy(ref, ref, sem).wait()

    def each_size(act):
        pl.when(jnp.logical_not(wide))(lambda: act(32))
        pl.when(wide)(lambda: act(36))

    def line_start(k, size):
        return jnp.where(south, ROWS - size * (k + 1), size * k)

    def turned(row):
        return jnp.where(south, line_rows - 1 - row, row)

    def send_lines(g):
        per = 3 * len(GROUPS[g])
        for pos, f in enumerate(GROUPS[g]):
            for s in range(3):
                src[g][pl.ds(3 * pos + s, ROWS, stride=per), :] = fields[f][0, :, 128 * s : 128 * (s + 1)]

        def to_line(k, size):
            start = line_start(k, size)
            send(
                src[g].at[pl.ds(start * per, size * per)], relay[g].at[pl.ds(0, size * per)],
                send_a.at[g, k], recv_a.at[g], member(3 * band + k, z, x_hi),
            )

        @pl.when(band < 2)
        def _():
            for k in range(3):
                to_line(k, 32)

        @pl.when(band == 2)
        def _():
            for k in range(2):
                to_line(k, 36)

    @pl.when(source)
    def _():
        for g in range(2):
            send_lines(g)

    right = jnp.where(lon == 31, 0, lon + 1)
    left = jnp.where(lon == 0, 31, lon - 1)

    @pl.when(stencil)
    def _():
        lane = lax.broadcasted_iota(jnp.int32, (ROWS, 128), 1)
        high = [ref[0, :, 256:384] for ref in fields]
        low = [ref[0, :, 0:128] for ref in fields]
        packed[0] = jnp.where(
            lane >= 124, high[0], jnp.where(lane >= 120, pltpu.roll(high[1], 124, 1), pltpu.roll(high[2], 120, 1))
        )
        packed[1] = jnp.where(lane < 4, low[0], jnp.where(lane < 8, pltpu.roll(low[1], 4, 1), pltpu.roll(low[2], 8, 1)))
        remote(packed.at[0], sides.at[0], send_s.at[0], recv_s.at[0], (lat, right))
        remote(packed.at[1], sides.at[1], send_s.at[1], recv_s.at[1], (lat, left))

    def owner(row):
        late = jnp.logical_and(wide, row >= 28)
        return jnp.where(late, 28 + lax.div(row - 28, 2), row), jnp.where(late, lax.rem(row, 2), 0)

    for g in range(2):
        per = 3 * len(GROUPS[g])
        each_size(lambda size, g=g, per=per: landed(relay[g].at[pl.ds(0, size * per)], recv_a.at[g]))

        def spread(row, carry, g=g, per=per):
            to, slot = owner(row)
            send(
                relay[g].at[pl.ds(turned(row) * per, per)], recv[g].at[pl.ds((32 * slot + slab) * per, per)],
                send_b.at[g], recv_b.at[g, slot], member(line, lax.div(to, 2), lax.rem(to, 2)),
            )
            return carry

        lax.fori_loop(0, line_rows, spread, 0)

    @pl.when(stencil)
    def _():
        landed(sides.at[0], recv_s.at[0])
        landed(sides.at[1], recv_s.at[1])
        lane = lax.broadcasted_iota(jnp.int32, (ROWS, 128), 1)
        for f in range(3):
            ext[f, 8 : 8 + ROWS, 0:CELLS] = fields[f][0]
            after, before = sides[1], sides[0]
            if f:
                after, before = pltpu.roll(after, 128 - 4 * f, 1), pltpu.roll(before, 4 * f, 1)
            ext[f, 8 : 8 + ROWS, CELLS : CELLS + 128] = jnp.where(lane < 64, after, before)

        @pl.when(lat > 2)
        def _():
            remote(ext.at[:, 8:16, :], ext.at[:, 104:112, :], send_r.at[0], recv_r.at[0], (lat - 1, lon))

        @pl.when(lat < 13)
        def _():
            remote(ext.at[:, 96:104, :], ext.at[:, 0:8, :], send_r.at[1], recv_r.at[1], (lat + 1, lon))

        @pl.when(lat == 2)
        def _():
            ext[:, 0:8, :] = jnp.zeros((3, 8, 512), F32)

        @pl.when(lat == 13)
        def _():
            ext[:, 104:112, :] = jnp.zeros((3, 8, 512), F32)

    up_line, up_place = lax.div(chain - 1, 32), lax.rem(chain + 31, 32)
    up = member(up_line, lax.div(up_place, 2), lax.rem(up_place, 2))
    up_count = jnp.where(jnp.logical_and(up_line >= 6, up_place >= 28), 2, 1)
    down_place = lax.rem(chain + 1, 32)
    down = member(lax.div(chain + 1, 32), lax.div(down_place, 2), lax.rem(down_place, 2))
    speed = speed_ref[0]

    def each_slot(act):
        act(0)
        pl.when(double)(lambda: act(1))

    @pl.when(chain == 0)
    def _():
        for e in range(4):
            nb[e, 0] = jnp.zeros((2 * HALF, 128), F32)

    @pl.when(chain == 255)
    def _():
        for e in range(4):
            nb[e, 3] = jnp.zeros((2 * HALF, 128), F32)

    def trade(e):
        @pl.when(chain > 0)
        def _():
            remote(nb.at[e, 1], nb.at[e, up_count + 1], send_x.at[e, 0], recv_x.at[e, 1], up)

        @pl.when(chain < 255)
        def _():
            remote(nb.at[e, count], nb.at[e, 0], send_x.at[e, 1], recv_x.at[e, 0], down)

    def traded(e):
        @pl.when(chain > 0)
        def _():
            landed(nb.at[e, 0], recv_x.at[e, 0])

        @pl.when(chain < 255)
        def _():
            landed(nb.at[e, count + 1], recv_x.at[e, 1])

    def transform(g, slot):
        per = 3 * len(GROUPS[g])
        grids = []
        for pos in range(len(GROUPS[g])):
            start = 32 * per * slot + 3 * pos
            grids.append(jnp.concatenate([recv[g][pl.ds(start + s, 32, stride=per), :] for s in range(3)], axis=0))
        mixed = outer_step(first_ref[...], jnp.concatenate(grids, axis=1))
        cos, sin = grid_ref[0], grid_ref[1]
        turned_rows = []
        for pos in range(len(GROUPS[g])):
            real, imag = mixed[:HALF, 128 * pos : 128 * (pos + 1)], mixed[HALF:, 128 * pos : 128 * (pos + 1)]
            turned_rows.append(jnp.concatenate([real * cos + imag * sin, imag * cos - real * sin], axis=1))
        spectrum = inner_step(fore_ref, jnp.concatenate(turned_rows, axis=0))
        return [
            (spectrum[HALF * pos : HALF * (pos + 1), :128], spectrum[HALF * pos : HALF * (pos + 1), 128:])
            for pos in range(len(GROUPS[g]))
        ]

    def restore(g, slot, spectra):
        per = 3 * len(GROUPS[g])
        cos, sin = grid_ref[0], grid_ref[1]
        back = inner_step(back_ref, jnp.concatenate([jnp.concatenate(pair, axis=1) for pair in spectra], axis=0))
        spun = []
        for pos in range(len(GROUPS[g])):
            real, imag = back[HALF * pos : HALF * (pos + 1), :128], back[HALF * pos : HALF * (pos + 1), 128:]
            spun.append(jnp.concatenate([real * cos - imag * sin, imag * cos + real * sin], axis=0))
        rows = outer_step(last_ref[...], jnp.concatenate(spun, axis=1))
        for pos in range(len(GROUPS[g])):
            for s in range(3):
                snd[g][pl.ds(32 * per * slot + 3 * pos + s, 32, stride=per), :] = rows[
                    32 * s : 32 * (s + 1), 128 * pos : 128 * (pos + 1)
                ]

    def put(ref, index, pair):
        ref[(*index, slice(0, HALF))] = pair[0]
        ref[(*index, slice(HALF, 2 * HALF))] = pair[1]

    def get(ref, *index):
        return ref[(*index, slice(0, HALF))], ref[(*index, slice(HALF, 2 * HALF))]

    def factors(slot):
        cosine = ring_ref[0, row0 + slot + 1]
        share = 1.0 / jnp.maximum(grid_ref[3], cosine)
        return share, share * cosine, SPIN * ring_ref[1, row0 + slot + 1]

    def push_east(slot, height, east, north):
        share, keep, spin = factors(slot)
        slope, swirl = share * (COURANT * grid_ref[2]), keep * spin
        return (
            east[0] + slope * height[1] + swirl * north[0],
            east[1] - slope * height[0] + swirl * north[1],
        )

    def push_north(slot, above, below, east, north):
        _, keep, spin = factors(slot)
        return tuple(
            north[p] - keep * ((0.5 * NORTH) * (below[p] - above[p]) + spin * east[p]) for p in range(2)
        )

    def push_height(slot, above, below, east, height):
        share, _, _ = factors(slot)
        share = speed * share
        slope = share * (COURANT * grid_ref[2])
        fall = share * (0.5 * NORTH)
        higher, lower = ring_ref[0, row0 + slot], ring_ref[0, row0 + slot + 2]
        return (
            height[0] + slope * east[1] - fall * (lower * below[0] - higher * above[0]),
            height[1] - slope * east[0] - fall * (lower * below[1] - higher * above[1]),
        )

    def first_height(slot):
        landed(recv[0].at[pl.ds(96 * slot, 96)], recv_b.at[0, slot])
        put(nb, (0, slot + 1), transform(0, slot)[0])

    def first_winds(slot):
        landed(recv[1].at[pl.ds(192 * slot, 192)], recv_b.at[1, slot])
        east, north = transform(1, slot)
        put(state, (slot, 0), east)
        put(state, (slot, 1), (flip * north[0], flip * north[1]))

    def north_one(slot):
        put(
            nb, (1, slot + 1),
            push_north(slot, get(nb, 0, slot), get(nb, 0, slot + 2), get(state, slot, 0), get(state, slot, 1)),
        )

    def east_one(slot):
        put(state, (slot, 2), push_east(slot, get(nb, 0, slot + 1), get(state, slot, 0), get(state, slot, 1)))

    def height_one(slot):
        put(
            nb, (2, slot + 1),
            push_height(slot, get(nb, 1, slot), get(nb, 1, slot + 2), get(state, slot, 2), get(nb, 0, slot + 1)),
        )

    def east_two(slot):
        put(state, (slot, 3), push_east(slot, get(nb, 2, slot + 1), get(state, slot, 2), get(nb, 1, slot + 1)))

    def north_two(slot):
        put(
            nb, (3, slot + 1),
            push_north(slot, get(nb, 2, slot), get(nb, 2, slot + 2), get(state, slot, 2), get(nb, 1, slot + 1)),
        )

    def winds_back(slot):
        north = get(nb, 3, slot + 1)
        restore(1, slot, [get(state, slot, 3), (flip * north[0], flip * north[1])])

    def height_back(slot):
        height = push_height(slot, get(nb, 3, slot), get(nb, 3, slot + 2), get(state, slot, 3), get(nb, 2, slot + 1))
        restore(0, slot, [height])

    def return_pieces(g, slot):
        per = 3 * len(GROUPS[g])
        row = turned(line_row + slot)

        def piece(d, carry):
            send(
                snd[g].at[pl.ds((32 * slot + d) * per, per)], home[g].at[pl.ds(row * per, per)],
                send_c.at[g, slot], recv_c.at[g], member(line, lax.rem(d, 16), lax.div(d, 16)),
            )
            return carry

        lax.fori_loop(0, 32, piece, 0)

    each_slot(first_height)
    trade(0)
    each_slot(first_winds)
    traded(0)
    each_slot(north_one)
    trade(1)
    each_slot(east_one)
    traded(1)
    each_slot(height_one)
    trade(2)
    each_slot(east_two)
    traded(2)
    each_slot(north_two)
    trade(3)
    each_slot(winds_back)
    each_slot(lambda slot: return_pieces(1, slot))
    traded(3)
    each_slot(height_back)
    each_slot(lambda slot: return_pieces(0, slot))

    to_band = jnp.where(wide, 2, lax.div(line, 3))
    to_lat = jnp.where(south, 15 - to_band, to_band)
    nth = line - 3 * to_band
    for g in (1, 0):
        per = 3 * len(GROUPS[g])

        def deliver(size, g=g, per=per):
            landed(home[g].at[pl.ds(0, size * per)], recv_c.at[g])
            start = line_start(nth, size)
            send(
                home[g].at[pl.ds(0, size * per)], ret[g].at[pl.ds(start * per, size * per)],
                send_d.at[g], recv_d.at[g, nth], (to_lat, slab),
            )

        each_size(deliver)

    @pl.when(stencil)
    def _():
        @pl.when(lat > 2)
        def _():
            landed(ext.at[:, 0:8, :], recv_r.at[1])

        @pl.when(lat < 13)
        def _():
            landed(ext.at[:, 104:112, :], recv_r.at[0])

        row = lax.broadcasted_iota(jnp.int32, (ROWS + 16, 128), 0) + (ROWS * lat - 8)
        latitude = (row.astype(F32) + (0.5 - NLAT // 2)) * (math.pi / NLAT)
        wide_cos = jnp.concatenate([jnp.cos(latitude)] * 4, axis=1)
        spin = jnp.concatenate([SPIN * jnp.sin(latitude)] * 4, axis=1)
        inverse = 1.0 / wide_cos
        east_scale = (0.5 * COURANT) * inverse

        def across(value):
            return pltpu.roll(value, 511, 1) - pltpu.roll(value, 1, 1)

        def along(value):
            return pltpu.roll(value, ROWS + 15, 0) - pltpu.roll(value, 1, 0)

        height, east, north = ext[0], ext[1], ext[2]
        for _step in range(2):
            east_inc = spin * north - east_scale * across(height)
            north_inc = (-0.5 * NORTH) * along(height) - spin * east
            east, north = east + east_inc, north + north_inc
            spread_out = east_scale * across(east) + (0.5 * NORTH) * inverse * along(north * wide_cos)
            height = height - speed * spread_out
        for out, value in zip(outs, (height, east, north)):
            out[0] = value[8 : 8 + ROWS, 0:CELLS]

    def arrived(k, size):
        for g in range(2):
            per = 3 * len(GROUPS[g])
            landed(ret[g].at[pl.ds(line_start(k, size) * per, size * per)], recv_d.at[g, k])

    def back(f, s):
        g = 0 if f == 0 else 1
        per, pos = 3 * len(GROUPS[g]), GROUPS[g].index(f)
        return ret[g][pl.ds(3 * pos + s, ROWS, stride=per), :]

    @pl.when(band < 2)
    def _():
        for k in range(3):
            arrived(k, 32)
        for f in range(3):
            for s in range(3):
                outs[f][0, :, 128 * s : 128 * (s + 1)] = back(f, s)

    @pl.when(band == 2)
    def _():
        for k in range(2):
            arrived(k, 36)
        row = lax.broadcasted_iota(jnp.int32, (ROWS, 128), 0)
        from_pole = jnp.where(south, ROWS - 1 - row, row) + 2 * ROWS
        for f in range(3):
            for s in range(3):
                lanes = slice(128 * s, 128 * (s + 1))
                outs[f][0, :, lanes] = jnp.where(from_pole < FINAL, back(f, s), outs[f][0, :, lanes])

    for g in range(2):
        per = 3 * len(GROUPS[g])

        def left_lines(size, lines, g=g, per=per):
            for k in range(lines):
                to = member(3 * band + k, z, x_hi)

                @pl.when(jnp.logical_not(jnp.logical_and(to[0] == lat, to[1] == lon)))
                def _(k=k):
                    landed(src[g].at[pl.ds(0, size * per)], send_a.at[g, k])

        pl.when(band < 2)(lambda f=left_lines: f(32, 3))
        pl.when(band == 2)(lambda f=left_lines: f(36, 2))

        pl.when(jnp.logical_not(wide))(lambda g=g, per=per: landed(relay[g].at[pl.ds(0, 31 * per)], send_b.at[g]))
        pl.when(jnp.logical_and(wide, jnp.logical_not(double)))(
            lambda g=g, per=per: landed(relay[g].at[pl.ds(0, 35 * per)], send_b.at[g])
        )
        pl.when(double)(lambda g=g, per=per: landed(relay[g].at[pl.ds(0, 34 * per)], send_b.at[g]))
        each_slot(lambda slot, g=g, per=per: landed(snd[g].at[pl.ds(0, 31 * per)], send_c.at[g, slot]))

        @pl.when(jnp.logical_not(jnp.logical_and(to_lat == lat, slab == lon)))
        def _(g=g, per=per):
            each_size(lambda size: landed(home[g].at[pl.ds(0, size * per)], send_d.at[g]))

    @pl.when(stencil)
    def _():
        for side in range(2):
            landed(packed.at[side], send_s.at[side])

        @pl.when(lat > 2)
        def _():
            landed(ext.at[:, 8:16, :], send_r.at[0])

        @pl.when(lat < 13)
        def _():
            landed(ext.at[:, 96:104, :], send_r.at[1])

    for e in range(4):
        pl.when(chain > 0)(lambda e=e: landed(nb.at[e, 1], send_x.at[e, 0]))
        pl.when(chain < 255)(lambda e=e: landed(nb.at[e, 1], send_x.at[e, 1]))


def body(height, east_wind, north_wind, wave_speed_sq):
    first, last, fore, back, grid, ring = tables()
    vmem, smem = pl.BlockSpec(memory_space=pltpu.VMEM), pl.BlockSpec(memory_space=pltpu.SMEM)
    block = jax.ShapeDtypeStruct((1, ROWS, CELLS), F32)
    pairs = []
    for rows in (ROWS, 36, 64, 64, 36, ROWS):
        pairs += [pltpu.VMEM((rows * 3 * len(group), 128), F32) for group in GROUPS]
    dma = pltpu.SemaphoreType.DMA
    return pl.pallas_call(
        kernel,
        out_shape=[block] * 3,
        in_specs=[vmem] * 3 + [smem] * 2 + [vmem] * 5,
        out_specs=[vmem] * 3,
        scratch_shapes=[
            *pairs,
            pltpu.VMEM((4, 4, 2 * HALF, 128), F32),
            pltpu.VMEM((2, 4, 2 * HALF, 128), F32),
            pltpu.VMEM((2, ROWS, 128), F32),
            pltpu.VMEM((2, ROWS, 128), F32),
            pltpu.VMEM((3, ROWS + 16, 512), F32),
            dma((2, 3)), dma((2,)), dma((2,)), dma((2, 2)), dma((2, 2)), dma((2,)), dma((2,)), dma((2, 3)),
            dma((4, 2)), dma((4, 2)), dma((2,)), dma((2,)), dma((2,)), dma((2,)),
        ],
        compiler_params=pltpu.CompilerParams(has_side_effects=True, vmem_limit_bytes=32 * 1024 * 1024),
        name="substeps",
    )(height, east_wind, north_wind, wave_speed_sq, ring, first, last, fore, back, grid)


def solution(mesh):
    block = P(None, "lat", "lon")
    return jax.shard_map(
        lambda *args: tuple(body(*args)),
        mesh=mesh, in_specs=(block, block, block, P()), out_specs=(block, block, block), check_vma=False,
    )
```

time: 671 us -> 80.3 us (0.12)
  the two profiles are of different devices: /device:TPU:1 before, /device:TPU:29 now
where the time goes in v1:
time: 80.3 us; the launch traced here: 79.9 us
  Pallas kernels  68.7 us (86%)
  local copies, waits for them, and re-layouts  9.96 us (12%)
  between operations  1.3 us (2%)
    pallas_call x1, Pallas kernels, body(): pl.pallas_call(kernel, out_shape=[block] * 3, in_specs=[vmem] * 3 + [smem...  68.7 us
    unnamed x21, local copies, waits for them, and re-layouts  9.96 us

profile of v1, /device:TPU:29, one launch (start us, length us, event | category | flops | bytes accessed | tf_op | source)
XLA Modules:
  0.0 79.9 jit_solution(9100029399621648288)
XLA Ops:
  1.3 0.0 copy-start
  1.3 0.9 %copy-done = bf16[2,256,256]{2,1,0:T(8,128)(2,1)S(1)} copy-done((bf16[2,256,256]{2,1,0:T(8,128)(2,1)S(1)}, bf16[2,256,256]{2,1,0:T(8,128)(2,1)}, u32[]{:S(2)}) %copy-start) | copy-done | bytes 262168
  2.2 0.0 copy-start.1
  2.2 0.9 %copy-done.1 = bf16[2,256,256]{2,1,0:T(8,128)(2,1)S(1)} copy-done((bf16[2,256,256]{2,1,0:T(8,128)(2,1)S(1)}, bf16[2,256,256]{2,1,0:T(8,128)(2,1)}, u32[]{:S(2)}) %copy-start.1) | copy-done | bytes 262168
  3.2 0.0 copy-start.2
  3.2 0.9 %copy-done.2 = f32[1,96,384]{2,1,0:T(8,128)S(1)} copy-done((f32[1,96,384]{2,1,0:T(8,128)S(1)}, f32[1,96,384]{2,1,0:T(8,128)}, u32[]{:S(2)}) %copy-start.2) | copy-done | bytes 147480
  4.1 0.0 copy-start.3
  4.1 0.9 %copy-done.3 = f32[1,96,384]{2,1,0:T(8,128)S(1)} copy-done((f32[1,96,384]{2,1,0:T(8,128)S(1)}, f32[1,96,384]{2,1,0:T(8,128)}, u32[]{:S(2)}) %copy-start.3) | copy-done | bytes 147480
  5.0 0.0 copy-start.4
  5.0 0.9 %copy-done.4 = f32[1,96,384]{2,1,0:T(8,128)S(1)} copy-done((f32[1,96,384]{2,1,0:T(8,128)S(1)}, f32[1,96,384]{2,1,0:T(8,128)}, u32[]{:S(2)}) %copy-start.4) | copy-done | bytes 147480
  5.9 0.0 copy-start.5
  5.9 0.9 %copy-done.5 = f32[4,56,128]{2,1,0:T(8,128)S(1)} copy-done((f32[4,56,128]{2,1,0:T(8,128)S(1)}, f32[4,56,128]{2,1,0:T(8,128)}, u32[]{:S(2)}) %copy-start.5) | copy-done | bytes 114712
  6.8 0.0 copy-start.6
  6.8 0.9 %copy-done.6 = bf16[112,288]{1,0:T(8,128)(2,1)S(1)} copy-done((bf16[112,288]{1,0:T(8,128)(2,1)S(1)}, bf16[112,288]{1,0:T(8,128)(2,1)}, u32[]{:S(2)}) %copy-start.6) | copy-done | bytes 64536
  7.7 0.0 copy-start.7
  7.7 0.9 %copy-done.7 = bf16[96,336]{1,0:T(8,128)(2,1)S(1)} copy-done((bf16[96,336]{1,0:T(8,128)(2,1)S(1)}, bf16[96,336]{1,0:T(8,128)(2,1)}, u32[]{:S(2)}) %copy-start.7) | copy-done | bytes 64536
  8.6 0.0 copy-start.8
  8.6 0.7 copy-done.8
  9.3 68.7 %substeps.1 = (f32[1,96,384]{2,1,0:T(8,128)S(1)}, f32[1,96,384]{2,1,0:T(8,128)S(1)}, f32[1,96,384]{2,1,0:T(8,128)S(1)}) custom-call(f32[1,96,384]{2,1,0:T(8,128)S(1)} %copy-done.2, f32[1,96,384]{2,1,0:T(8,128)S(1)} %copy-done.3, f32[1,96,384]{2,1,0:T(8,128)S(1)} %copy-done.4, f32[1]{0:T(128)S(6)} %copy.16.speed_ref, f32[2,266]{1,0:T(2,128)S(1)} %copy-done.8, ...), custom_call_target="tpu_custom_call" | custom-call | tf_op jit(solution)/shard_map/substeps/pallas_call | solution.py:554
  77.9 0.7 copy.17
  78.6 0.7 copy.18
  79.3 0.7 copy.19
Async XLA Ops:
  1.3 1.0 %copy-start = (bf16[2,256,256]{2,1,0:T(8,128)(2,1)S(1)}, bf16[2,256,256]{2,1,0:T(8,128)(2,1)}, u32[]{:S(2)}) copy-start(bf16[2,256,256]{2,1,0:T(8,128)(2,1)} %constant.16.clone.back_ref) | copy-start | bytes 786436
  2.2 0.9 %copy-start.1 = (bf16[2,256,256]{2,1,0:T(8,128)(2,1)S(1)}, bf16[2,256,256]{2,1,0:T(8,128)(2,1)}, u32[]{:S(2)}) copy-start(bf16[2,256,256]{2,1,0:T(8,128)(2,1)} %constant.15.clone.fore_ref) | copy-start | bytes 786436
  3.2 0.9 %copy-start.2 = (f32[1,96,384]{2,1,0:T(8,128)S(1)}, f32[1,96,384]{2,1,0:T(8,128)}, u32[]{:S(2)}) copy-start(f32[1,96,384]{2,1,0:T(8,128)} %h_ref.1) | copy-start | bytes 442372
  4.1 0.9 %copy-start.3 = (f32[1,96,384]{2,1,0:T(8,128)S(1)}, f32[1,96,384]{2,1,0:T(8,128)}, u32[]{:S(2)}) copy-start(f32[1,96,384]{2,1,0:T(8,128)} %u_ref.1) | copy-start | bytes 442372
  5.0 0.9 %copy-start.4 = (f32[1,96,384]{2,1,0:T(8,128)S(1)}, f32[1,96,384]{2,1,0:T(8,128)}, u32[]{:S(2)}) copy-start(f32[1,96,384]{2,1,0:T(8,128)} %v_ref.1) | copy-start | bytes 442372
  5.9 0.9 %copy-start.5 = (f32[4,56,128]{2,1,0:T(8,128)S(1)}, f32[4,56,128]{2,1,0:T(8,128)}, u32[]{:S(2)}) copy-start(f32[4,56,128]{2,1,0:T(8,128)} %constant.17.clone.grid_ref) | copy-start | bytes 344068
  6.8 0.9 %copy-start.6 = (bf16[112,288]{1,0:T(8,128)(2,1)S(1)}, bf16[112,288]{1,0:T(8,128)(2,1)}, u32[]{:S(2)}) copy-start(bf16[112,288]{1,0:T(8,128)(2,1)} %constant.13.clone.first_ref) | copy-start | bytes 193540
  7.7 0.9 %copy-start.7 = (bf16[96,336]{1,0:T(8,128)(2,1)S(1)}, bf16[96,336]{1,0:T(8,128)(2,1)}, u32[]{:S(2)}) copy-start(bf16[96,336]{1,0:T(8,128)(2,1)} %constant.14.clone.last_ref) | copy-start | bytes 193540
  8.6 0.7 copy-start.8

commit v2 on v1

--- a/solution.py
+++ b/solution.py
@@ -50,16 +50,12 @@
     forward_high, forward_low = split(forward)
     backward_high, backward_low = split(backward)
     grid = np.stack([np.cos(turn), np.sin(turn), steep, half_sine]).astype(np.float32)
-    row = np.arange(-1, LAST + 1)
-    latitude = -0.5 * np.pi + (row + 0.5) * np.pi / NLAT
-    ring = np.stack([np.cos(latitude), np.sin(latitude)]).astype(np.float32)
     return (
         np.concatenate([first_high, first_low, first_high], axis=1),
         np.concatenate([last_high, last_low, last_high], axis=1),
         np.stack([forward_high, forward_low]),
         np.stack([backward_high, backward_low]),
         grid,
-        ring,
     )
 
 
@@ -74,23 +70,27 @@
 
 def outer_step(table, value):
     high, low = parts(value)
-    return dot(table, jnp.concatenate([high, high, low], axis=0))
+    return dot(table.astype(BF16), jnp.concatenate([high, high, low], axis=0))
 
 
 def inner_step(table, value):
     high, low = parts(value)
-    return dot(high, table[0]) + dot(low, table[0]) + dot(high, table[1])
+    table_high, table_low = table[0].astype(BF16), table[1].astype(BF16)
+    return dot(high, table_high) + dot(low, table_high) + dot(high, table_low)
 
 
 def kernel(
-    h_ref, u_ref, v_ref, speed_ref, ring_ref, first_ref, last_ref, fore_ref, back_ref, grid_ref,
+    speed_ref, h_hbm, u_hbm, v_hbm, first_hbm, last_hbm, fore_hbm, back_hbm, grid_hbm,
     h_out, u_out, v_out,
+    h_ref, u_ref, v_ref, first_ref, last_ref, fore_ref, back_ref, grid_ref,
     src0, src1, relay0, relay1, recv0, recv1, snd0, snd1, home0, home1, ret0, ret1,
     nb, state, packed, sides, ext,
-    send_a, recv_a, send_b, recv_b, send_c, recv_c, send_d, recv_d,
+    loads, send_a, recv_a, send_b, recv_b, send_c, recv_c, send_d, recv_d,
     send_x, recv_x, send_s, recv_s, send_r, recv_r,
 ):
     fields, outs = (h_ref, u_ref, v_ref), (h_out, u_out, v_out)
+    operands = (h_hbm, u_hbm, v_hbm, first_hbm, last_hbm, fore_hbm, back_hbm, grid_hbm)
+    held = (h_ref, u_ref, v_ref, first_ref, last_ref, fore_ref, back_ref, grid_ref)
     src, relay, recv = (src0, src1), (relay0, relay1), (recv0, recv1)
     snd, home, ret = (snd0, snd1), (home0, home1), (ret0, ret1)
     lat, lon = lax.axis_index("lat"), lax.axis_index("lon")
@@ -118,6 +118,14 @@
         to_band = 4 * lax.div(to_line, 4) + 2 * lax.rem(to_x, 2) + to_core
         return jnp.where(south, 15 - to_band, to_band), 16 * lax.div(to_x, 2) + to_z
 
+    def mate(to_place):
+        shift = lax.rem(to_place, 2) - core
+        return jnp.where(south, lat - shift, lat + shift), 16 * x_hi + lax.div(to_place, 2)
+
+    def around(k, here, total):
+        step = lax.div(k + 1, 2)
+        return lax.rem(here + total + jnp.where(lax.rem(k, 2) == 1, step, -step), total)
+
     def send(here, there, send_sem, recv_sem, target):
         same = jnp.logical_and(target[0] == lat, target[1] == lon)
 
@@ -149,11 +157,61 @@
     def turned(row):
         return jnp.where(south, line_rows - 1 - row, row)
 
-    def send_lines(g):
+    right = jnp.where(lon == 31, 0, lon + 1)
+    left = jnp.where(lon == 0, 31, lon - 1)
+    up_line, up_place = lax.div(chain + 31, 32) - 1, lax.rem(chain + 31, 32)
+    up = member(up_line, lax.div(up_place, 2), lax.rem(up_place, 2))
+    up_count = jnp.where(jnp.logical_and(up_line >= 6, up_place >= 28), 2, 1)
+    down_place = lax.rem(chain + 1, 32)
+    down = member(lax.div(chain + 1, 32), lax.div(down_place, 2), lax.rem(down_place, 2))
+    to_band = jnp.where(wide, 2, lax.div(line, 3))
+    to_lat = jnp.where(south, 15 - to_band, to_band)
+    nth = line - 3 * to_band
+
+    barrier = pltpu.get_barrier_semaphore()
+
+    def greet(target):
+        pl.semaphore_signal(barrier, inc=1, device_id=target, device_id_type=MESH)
+
+    def greet_other(target):
+        other = jnp.logical_not(jnp.logical_and(target[0] == lat, target[1] == lon))
+        pl.when(other)(lambda: greet(target))
+        return other.astype(jnp.int32)
+
+    def greet_mate(k, carry):
+        greet(mate(lax.rem(place + k, 32)))
+        return carry
+
+    greeted = 31 + greet_other((to_lat, slab))
+    for k in range(3):
+        target = member(jnp.minimum(3 * band + k, 7), z, x_hi)
+        other = jnp.logical_not(jnp.logical_and(target[0] == lat, target[1] == lon))
+        meant = jnp.logical_and(other, jnp.logical_or(band < 2, jnp.logical_and(band == 2, k < 2)))
+        pl.when(meant)(lambda target=target: greet(target))
+        greeted += meant.astype(jnp.int32)
+    for meant, target in (
+        (chain > 0, up), (chain < 255, down), (stencil, (lat, left)), (stencil, (lat, right)),
+        (jnp.logical_and(stencil, lat > 2), (lat - 1, lon)), (jnp.logical_and(stencil, lat < 13), (lat + 1, lon)),
+    ):
+        pl.when(meant)(lambda target=target: greet(target))
+        greeted += meant.astype(jnp.int32)
+    lax.fori_loop(1, 32, greet_mate, 0)
+
+    for index, (there, here) in enumerate(zip(operands, held)):
+        pltpu.make_async_copy(there, here, loads.at[index]).start()
+
+    def loaded(*indices):
+        for index in indices:
+            pltpu.make_async_copy(operands[index], held[index], loads.at[index]).wait()
+
+    def gather_lines(g):
         per = 3 * len(GROUPS[g])
         for pos, f in enumerate(GROUPS[g]):
             for s in range(3):
                 src[g][pl.ds(3 * pos + s, ROWS, stride=per), :] = fields[f][0, :, 128 * s : 128 * (s + 1)]
+
+    def send_lines(g):
+        per = 3 * len(GROUPS[g])
 
         def to_line(k, size):
             start = line_start(k, size)
@@ -172,13 +230,16 @@
             for k in range(2):
                 to_line(k, 36)
 
+    loaded(0)
+    pl.when(source)(lambda: gather_lines(0))
+    pl.semaphore_wait(barrier, greeted)
+    pl.when(source)(lambda: send_lines(0))
+    loaded(1, 2)
+
     @pl.when(source)
     def _():
-        for g in range(2):
-            send_lines(g)
-
-    right = jnp.where(lon == 31, 0, lon + 1)
-    left = jnp.where(lon == 0, 31, lon - 1)
+        gather_lines(1)
+        send_lines(1)
 
     @pl.when(stencil)
     def _():
@@ -200,15 +261,33 @@
         per = 3 * len(GROUPS[g])
         each_size(lambda size, g=g, per=per: landed(relay[g].at[pl.ds(0, size * per)], recv_a.at[g]))
 
-        def spread(row, carry, g=g, per=per):
+        def spread(k, carry, g=g, per=per):
+            row = around(k, line_row, line_rows)
             to, slot = owner(row)
             send(
                 relay[g].at[pl.ds(turned(row) * per, per)], recv[g].at[pl.ds((32 * slot + slab) * per, per)],
-                send_b.at[g], recv_b.at[g, slot], member(line, lax.div(to, 2), lax.rem(to, 2)),
+                send_b.at[g], recv_b.at[g, slot], mate(to),
             )
             return carry
 
-        lax.fori_loop(0, line_rows, spread, 0)
+        def spread_one(k, carry, g=g, per=per):
+            to = around(k, place, 32)
+            remote(
+                relay[g].at[pl.ds(turned(to) * per, per)], recv[g].at[pl.ds(slab * per, per)],
+                send_b.at[g], recv_b.at[g, 0], mate(to),
+            )
+            return carry
+
+        @pl.when(wide)
+        def _(spread=spread):
+            lax.fori_loop(0, 36, spread, 0)
+
+        @pl.when(jnp.logical_not(wide))
+        def _(g=g, per=per, spread_one=spread_one):
+            pltpu.make_async_copy(
+                relay[g].at[pl.ds(turned(place) * per, per)], recv[g].at[pl.ds(slab * per, per)], recv_b.at[g, 0]
+            ).start()
+            lax.fori_loop(1, 32, spread_one, 0)
 
     @pl.when(stencil)
     def _():
@@ -238,11 +317,7 @@
         def _():
             ext[:, 104:112, :] = jnp.zeros((3, 8, 512), F32)
 
-    up_line, up_place = lax.div(chain - 1, 32), lax.rem(chain + 31, 32)
-    up = member(up_line, lax.div(up_place, 2), lax.rem(up_place, 2))
-    up_count = jnp.where(jnp.logical_and(up_line >= 6, up_place >= 28), 2, 1)
-    down_place = lax.rem(chain + 1, 32)
-    down = member(lax.div(chain + 1, 32), lax.div(down_place, 2), lax.rem(down_place, 2))
+    loaded(3, 4, 5, 6, 7)
     speed = speed_ref[0]
 
     def each_slot(act):
@@ -317,10 +392,14 @@
     def get(ref, *index):
         return ref[(*index, slice(0, HALF))], ref[(*index, slice(HALF, 2 * HALF))]
 
+    def polar(row):
+        return (jnp.full((1, 128), row, jnp.int32).astype(F32) + 0.5) * (math.pi / NLAT)
+
     def factors(slot):
-        cosine = ring_ref[0, row0 + slot + 1]
+        angle = polar(row0 + slot)
+        cosine = jnp.sin(angle)
         share = 1.0 / jnp.maximum(grid_ref[3], cosine)
-        return share, share * cosine, SPIN * ring_ref[1, row0 + slot + 1]
+        return share, share * cosine, -SPIN * jnp.cos(angle)
 
     def push_east(slot, height, east, north):
         share, keep, spin = factors(slot)
@@ -341,7 +420,7 @@
         share = speed * share
         slope = share * (COURANT * grid_ref[2])
         fall = share * (0.5 * NORTH)
-        higher, lower = ring_ref[0, row0 + slot], ring_ref[0, row0 + slot + 2]
+        higher, lower = jnp.sin(polar(row0 + slot - 1)), jnp.sin(polar(row0 + slot + 1))
         return (
             height[0] + slope * east[1] - fall * (lower * below[0] - higher * above[0]),
             height[1] - slope * east[0] - fall * (lower * below[1] - higher * above[1]),
@@ -393,14 +472,19 @@
         per = 3 * len(GROUPS[g])
         row = turned(line_row + slot)
 
-        def piece(d, carry):
-            send(
+        def piece(k, carry):
+            to = around(k, place, 32)
+            d = 16 * lax.rem(to, 2) + lax.div(to, 2)
+            remote(
                 snd[g].at[pl.ds((32 * slot + d) * per, per)], home[g].at[pl.ds(row * per, per)],
-                send_c.at[g, slot], recv_c.at[g], member(line, lax.rem(d, 16), lax.div(d, 16)),
+                send_c.at[g, slot], recv_c.at[g], mate(to),
             )
             return carry
 
-        lax.fori_loop(0, 32, piece, 0)
+        pltpu.make_async_copy(
+            snd[g].at[pl.ds((32 * slot + slab) * per, per)], home[g].at[pl.ds(row * per, per)], recv_c.at[g]
+        ).start()
+        lax.fori_loop(1, 32, piece, 0)
 
     each_slot(first_height)
     trade(0)
@@ -422,9 +506,6 @@
     each_slot(height_back)
     each_slot(lambda slot: return_pieces(0, slot))
 
-    to_band = jnp.where(wide, 2, lax.div(line, 3))
-    to_lat = jnp.where(south, 15 - to_band, to_band)
-    nth = line - 3 * to_band
     for g in (1, 0):
         per = 3 * len(GROUPS[g])
 
@@ -544,8 +625,7 @@
 
 
 def body(height, east_wind, north_wind, wave_speed_sq):
-    first, last, fore, back, grid, ring = tables()
-    vmem, smem = pl.BlockSpec(memory_space=pltpu.VMEM), pl.BlockSpec(memory_space=pltpu.SMEM)
+    constants = [np.asarray(table, np.float32) for table in tables()]
     block = jax.ShapeDtypeStruct((1, ROWS, CELLS), F32)
     pairs = []
     for rows in (ROWS, 36, 64, 64, 36, ROWS):
@@ -554,21 +634,25 @@
     return pl.pallas_call(
         kernel,
         out_shape=[block] * 3,
-        in_specs=[vmem] * 3 + [smem] * 2 + [vmem] * 5,
-        out_specs=[vmem] * 3,
+        in_specs=[pl.BlockSpec(memory_space=pltpu.SMEM)] + [pl.BlockSpec(memory_space=pl.ANY)] * 8,
+        out_specs=[pl.BlockSpec(memory_space=pltpu.VMEM)] * 3,
         scratch_shapes=[
+            *[pltpu.VMEM((1, ROWS, CELLS), F32)] * 3,
+            *[pltpu.VMEM(table.shape, table.dtype) for table in constants],
             *pairs,
             pltpu.VMEM((4, 4, 2 * HALF, 128), F32),
             pltpu.VMEM((2, 4, 2 * HALF, 128), F32),
             pltpu.VMEM((2, ROWS, 128), F32),
             pltpu.VMEM((2, ROWS, 128), F32),
             pltpu.VMEM((3, ROWS + 16, 512), F32),
-            dma((2, 3)), dma((2,)), dma((2,)), dma((2, 2)), dma((2, 2)), dma((2,)), dma((2,)), dma((2, 3)),
+            dma((8,)), dma((2, 3)), dma((2,)), dma((2,)), dma((2, 2)), dma((2, 2)), dma((2,)), dma((2,)), dma((2, 3)),
             dma((4, 2)), dma((4, 2)), dma((2,)), dma((2,)), dma((2,)), dma((2,)),
         ],
-        compiler_params=pltpu.CompilerParams(has_side_effects=True, vmem_limit_bytes=32 * 1024 * 1024),
+        compiler_params=pltpu.CompilerParams(
+            collective_id=0, has_side_effects=True, vmem_limit_bytes=60 * 1024 * 1024
+        ),
         name="substeps",
-    )(height, east_wind, north_wind, wave_speed_sq, ring, first, last, fore, back, grid)
+    )(wave_speed_sq, height, east_wind, north_wind, *constants)
 
 
 def solution(mesh):

time: 80.3 us -> 65.7 us (0.82)
  the two profiles are of different devices: /device:TPU:29 before, /device:TPU:1 now
where the time goes in v2:
time: 65.7 us; the launch traced here: 65.6 us
  Pallas kernels  61 us (93%)
  local copies, waits for them, and re-layouts  3.25 us (5%)
  between operations  1.3 us (2%)
    pallas_call x1, Pallas kernels, body(): pl.pallas_call(kernel, out_shape=[block] * 3, in_specs=[pl.BlockSpec(memo...  61 us
    unnamed x7, local copies, waits for them, and re-layouts  3.25 us

profile of v2, /device:TPU:1, one launch (start us, length us, event | category | flops | bytes accessed | tf_op | source)
XLA Modules:
  0.0 65.6 jit_solution(11032926937360108860)
XLA Ops:
  1.3 61.0 %substeps.1 = (f32[1,96,384]{2,1,0:T(8,128)}, f32[1,96,384]{2,1,0:T(8,128)}, f32[1,96,384]{2,1,0:T(8,128)}) custom-call(f32[1]{0:T(128)S(6)} %copy.15.speed_ref, f32[1,96,384]{2,1,0:T(8,128)} %h_hbm.1, f32[1,96,384]{2,1,0:T(8,128)} %u_hbm.1, f32[1,96,384]{2,1,0:T(8,128)} %v_hbm.1, f32[112,288]{1,0:T(8,128)} %constant.10.clone.first_hbm, ...), custom_call_target="tpu_custom_call" | custom-call | tf_op jit(solution)/shard_map/substeps/pallas_call | solution.py:634
  62.3 0.0 copy-start.1
  62.3 1.6 %copy.16 = f32[1,96,384]{2,1,0:T(8,128)} copy(f32[1,96,384]{2,1,0:T(8,128)} %get-tuple-element.6) | data formatting | bytes 294912
  63.9 0.0 copy-done.1
  63.9 0.0 copy-start
  63.9 0.7 %copy.17 = f32[1,96,384]{2,1,0:T(8,128)} copy(f32[1,96,384]{2,1,0:T(8,128)S(1)} %copy-done.1) | data formatting | bytes 294912
  64.6 0.3 copy-done
  64.9 0.7 %copy.18 = f32[1,96,384]{2,1,0:T(8,128)} copy(f32[1,96,384]{2,1,0:T(8,128)S(1)} %copy-done) | data formatting | bytes 294912
Async XLA Ops:
  62.3 1.6 %copy-start.1 = (f32[1,96,384]{2,1,0:T(8,128)S(1)}, f32[1,96,384]{2,1,0:T(8,128)}, u32[]{:S(2)}) copy-start(f32[1,96,384]{2,1,0:T(8,128)} %get-tuple-element.7) | copy-start | bytes 442372
  63.9 1.0 %copy-start = (f32[1,96,384]{2,1,0:T(8,128)S(1)}, f32[1,96,384]{2,1,0:T(8,128)}, u32[]{:S(2)}) copy-start(f32[1,96,384]{2,1,0:T(8,128)} %get-tuple-element.8) | copy-start | bytes 442372

commit v3 on v1

v3 whole, which is shorter than its diff:
```python
import math

import jax
import jax.numpy as jnp
import ml_dtypes
import numpy as np
from jax import lax
from jax.experimental import pallas as pl
from jax.experimental.pallas import tpu as pltpu
from jax.sharding import PartitionSpec as P

NLON, NLAT = 12288, 1536
ROWS, CELLS = 96, 384
OUTER, INNER = 96, 128
HALF = 56
COURANT, SPIN = 0.45, 0.3
NORTH = COURANT * 2.0 * NLAT / NLON
FINAL = 260
HOLD = 3
OWNERS = 88
WINGS = HOLD + 2
MESH = pl.DeviceIdType.MESH
F32, BF16 = jnp.float32, jnp.bfloat16
GROUPS = ((0,), (1, 2))


def split(table):
    high = table.astype(ml_dtypes.bfloat16)
    low = (table - high.astype(np.float64)).astype(ml_dtypes.bfloat16)
    return high, low


def tables():
    a = np.array([3 * d + s for s in range(3) for d in range(32)])
    k1 = np.arange(HALF)
    live = (k1 <= OUTER // 2).astype(np.float64)
    angle = 2 * np.pi * ((k1[:, None] * a[None, :]) % OUTER) / OUTER
    first = np.concatenate([np.cos(angle) * live[:, None], -np.sin(angle) * live[:, None]], axis=0)
    weight = live * np.where((k1 == 0) | (k1 == OUTER // 2), 1.0, 2.0) / NLON
    last = np.concatenate([np.cos(angle) * weight[:, None], -np.sin(angle) * weight[:, None]], axis=0).T
    n = np.arange(INNER)
    turn = 2 * np.pi * (k1[:, None] * n[None, :]) / NLON
    inner = 2 * np.pi * ((n[:, None] * n[None, :]) % INNER) / INNER
    cos, sin = np.cos(inner), np.sin(inner)
    forward = np.block([[cos, -sin], [sin, cos]])
    backward = np.block([[cos, sin], [-sin, cos]])
    wave = k1[:, None] + OUTER * n[None, :]
    steep = np.sin(2 * np.pi * wave / NLON) * live[:, None]
    half_sine = np.where(live[:, None] > 0, 0.5 * np.abs(np.sin(np.pi * wave / NLON)), 1.0)
    first_high, first_low = split(first)
    last_high, last_low = split(last)
    forward_high, forward_low = split(forward)
    backward_high, backward_low = split(backward)
    grid = np.stack([np.cos(turn), np.sin(turn), steep, half_sine]).astype(np.float32)
    return (
        np.concatenate([first_high, first_low, first_high], axis=1),
        np.concatenate([last_high, last_low, last_high], axis=1),
        np.stack([forward_high, forward_low]),
        np.stack([backward_high, backward_low]),
        grid,
    )


def parts(value):
    high = value.astype(BF16)
    return high, (value - high.astype(F32)).astype(BF16)


def dot(left, right):
    return jnp.dot(left, right, preferred_element_type=F32)


def outer_step(table, value):
    high, low = parts(value)
    return dot(table.astype(BF16), jnp.concatenate([high, high, low], axis=0))


def inner_step(table, value):
    high, low = parts(value)
    table_high, table_low = table[0].astype(BF16), table[1].astype(BF16)
    return dot(high, table_high) + dot(low, table_high) + dot(high, table_low)


def kernel(
    speed_ref, h_hbm, u_hbm, v_hbm, first_hbm, last_hbm, fore_hbm, back_hbm, grid_hbm,
    h_out, u_out, v_out,
    h_ref, u_ref, v_ref, first_ref, last_ref, fore_ref, back_ref, grid_ref,
    src0, src1, recv0, recv1, snd0, snd1, ret0, ret1,
    tall, tall_new, wind, wind_new, wind_last, scale, packed, sides, ext,
    loads, send_a, recv_a, send_c, recv_c, send_x, recv_x, send_s, recv_s, send_r, recv_r,
):
    fields, outs = (h_ref, u_ref, v_ref), (h_out, u_out, v_out)
    operands = (h_hbm, u_hbm, v_hbm, first_hbm, last_hbm, fore_hbm, back_hbm, grid_hbm)
    held = (h_ref, u_ref, v_ref, first_ref, last_ref, fore_ref, back_ref, grid_ref)
    src, recv, snd, ret = (src0, src1), (recv0, recv1), (snd0, snd1), (ret0, ret1)
    lat, lon = lax.axis_index("lat"), lax.axis_index("lon")
    south = lat >= 8
    band = jnp.where(south, 15 - lat, lat)
    core = lax.rem(band, 2)
    z = lax.rem(lon, 16)
    x = 2 * lax.div(lon, 16) + lax.rem(lax.div(band, 2), 2)
    line = jnp.where(band < 4, x, 7 - x)
    step = lax.rem(z + line, 16) + jnp.where(lax.rem(z + line, 16) < lax.rem(10 * line + line, 16), 16, 0)
    nth = step - lax.rem(11 * line, 16)
    owner = jnp.logical_and(core == 1, nth < 11)
    chain = 11 * line + nth
    source = band <= 2
    stencil = band >= 2
    partners = jnp.where(band < 2, 32, 24)
    my_band = jnp.minimum(lax.div(chain, 32), 2)
    my_lat = jnp.where(south, 15 - my_band, my_band)

    def holder(n):
        to_line = lax.div(n, 11)
        to_x = jnp.where(to_line < 4, to_line, 7 - to_line)
        to_band = 4 * lax.div(to_line, 4) + 2 * lax.rem(to_x, 2) + 1
        return jnp.where(south, 15 - to_band, to_band), 16 * lax.div(to_x, 2) + lax.rem(n + 16 - to_line, 16)

    def same(target):
        return jnp.logical_and(target[0] == lat, target[1] == lon)

    def remote(here, there, send_sem, recv_sem, target):
        pltpu.make_async_remote_copy(
            src_ref=here, dst_ref=there, send_sem=send_sem, recv_sem=recv_sem, device_id=target, device_id_type=MESH
        ).start()

    def send(here, there, send_sem, recv_sem, target):
        own = same(target)

        @pl.when(own)
        def _():
            pltpu.make_async_copy(here, there, recv_sem).start()

        @pl.when(jnp.logical_not(own))
        def _():
            remote(here, there, send_sem, recv_sem, target)

    def landed(ref, sem):
        pltpu.make_async_copy(ref, ref, sem).wait()

    def first_row(i):
        return jnp.where(south, ROWS - HOLD - HOLD * i, HOLD * i)

    right = jnp.where(lon == 31, 0, lon + 1)
    left = jnp.where(lon == 0, 31, lon - 1)
    before = chain + jnp.where(south, 1, -1)
    after = chain + jnp.where(south, -1, 1)
    has_before = jnp.logical_and(owner, jnp.logical_and(before >= 0, before < OWNERS))
    has_after = jnp.logical_and(owner, jnp.logical_and(after >= 0, after < OWNERS))
    before_device, after_device = holder(jnp.maximum(before, 0)), holder(jnp.maximum(after, 0))

    barrier = pltpu.get_barrier_semaphore()

    def greet(target):
        pl.semaphore_signal(barrier, inc=1, device_id=target, device_id_type=MESH)

    def greet_other(target):
        pl.when(jnp.logical_not(same(target)))(lambda: greet(target))

    def target_of(k):
        return lax.rem(lon + k, partners)

    def greet_holder(k, carry):
        greet_other(holder(32 * band + k))
        return carry

    def greet_source(k, carry):
        greet_other((my_lat, k))
        return carry

    @pl.when(owner)
    def _():
        lax.fori_loop(0, 32, greet_source, 0)

    @pl.when(source)
    def _():
        lax.fori_loop(0, partners, greet_holder, 0)

    own_rows = jnp.logical_and(jnp.logical_and(owner, source), my_band == band)
    greeted = jnp.where(owner, 32, 0) + jnp.where(source, partners, 0) - jnp.where(own_rows, 2, 0)
    for meant, target in (
        (has_before, before_device), (has_after, after_device), (stencil, (lat, left)), (stencil, (lat, right)),
        (jnp.logical_and(stencil, lat > 2), (lat - 1, lon)), (jnp.logical_and(stencil, lat < 13), (lat + 1, lon)),
    ):
        pl.when(meant)(lambda target=target: greet(target))
        greeted += meant.astype(jnp.int32)

    def load(*indices):
        for index in indices:
            pltpu.make_async_copy(operands[index], held[index], loads.at[index]).start()

    def loaded(*indices):
        for index in indices:
            pltpu.make_async_copy(operands[index], held[index], loads.at[index]).wait()

    load(0, 1, 2)
    pl.when(owner)(lambda: load(3, 4, 5, 6, 7))

    def gather(g):
        per = 3 * len(GROUPS[g])
        for pos, f in enumerate(GROUPS[g]):
            for s in range(3):
                src[g][pl.ds(3 * pos + s, ROWS, stride=per), :] = fields[f][0, :, 128 * s : 128 * (s + 1)]

    def send_rows(g):
        size = HOLD * 3 * len(GROUPS[g])

        def one(k, carry):
            i = target_of(k)
            send(
                src[g].at[pl.ds(first_row(i) * (size // HOLD), size)], recv[g].at[pl.ds(lon * size, size)],
                send_a.at[g], recv_a.at[g], holder(32 * band + i),
            )
            return carry

        lax.fori_loop(0, partners, one, 0)

    loaded(0)
    pl.when(source)(lambda: gather(0))
    pl.semaphore_wait(barrier, greeted)
    pl.when(source)(lambda: send_rows(0))
    loaded(1, 2)

    @pl.when(source)
    def _():
        gather(1)
        send_rows(1)

    @pl.when(stencil)
    def _():
        lane = lax.broadcasted_iota(jnp.int32, (ROWS, 128), 1)
        high = [ref[0, :, 256:384] for ref in fields]
        low = [ref[0, :, 0:128] for ref in fields]
        packed[0] = jnp.where(
            lane >= 124, high[0], jnp.where(lane >= 120, pltpu.roll(high[1], 124, 1), pltpu.roll(high[2], 120, 1))
        )
        packed[1] = jnp.where(lane < 4, low[0], jnp.where(lane < 8, pltpu.roll(low[1], 4, 1), pltpu.roll(low[2], 8, 1)))
        remote(packed.at[0], sides.at[0], send_s.at[0], recv_s.at[0], (lat, right))
        remote(packed.at[1], sides.at[1], send_s.at[1], recv_s.at[1], (lat, left))

    @pl.when(stencil)
    def _():
        landed(sides.at[0], recv_s.at[0])
        landed(sides.at[1], recv_s.at[1])
        lane = lax.broadcasted_iota(jnp.int32, (ROWS, 128), 1)
        for f in range(3):
            ext[f, 8 : 8 + ROWS, 0:CELLS] = fields[f][0]
            east_side, west_side = sides[1], sides[0]
            if f:
                east_side, west_side = pltpu.roll(east_side, 128 - 4 * f, 1), pltpu.roll(west_side, 4 * f, 1)
            ext[f, 8 : 8 + ROWS, CELLS : CELLS + 128] = jnp.where(lane < 64, east_side, west_side)

        @pl.when(lat > 2)
        def _():
            remote(ext.at[:, 8:16, :], ext.at[:, 104:112, :], send_r.at[0], recv_r.at[0], (lat - 1, lon))

        @pl.when(lat < 13)
        def _():
            remote(ext.at[:, 96:104, :], ext.at[:, 0:8, :], send_r.at[1], recv_r.at[1], (lat + 1, lon))

        @pl.when(lat == 2)
        def _():
            ext[:, 0:8, :] = jnp.zeros((3, 8, 512), F32)

        @pl.when(lat == 13)
        def _():
            ext[:, 104:112, :] = jnp.zeros((3, 8, 512), F32)

    def transform(g):
        size = HOLD * 3 * len(GROUPS[g])
        order = [(row, pos) for row in range(HOLD) for pos in range(len(GROUPS[g]))]
        grids = [
            jnp.concatenate(
                [recv[g][pl.ds(row * (size // HOLD) + 3 * pos + s, 32, stride=size), :] for s in range(3)], axis=0
            )
            for row, pos in order
        ]
        mixed = outer_step(first_ref[...], jnp.concatenate(grids, axis=1))
        cos, sin = grid_ref[0], grid_ref[1]
        twisted = []
        for n in range(len(order)):
            real, imag = mixed[:HALF, 128 * n : 128 * (n + 1)], mixed[HALF:, 128 * n : 128 * (n + 1)]
            twisted.append(jnp.concatenate([real * cos + imag * sin, imag * cos - real * sin], axis=1))
        spectrum = inner_step(fore_ref, jnp.concatenate(twisted, axis=0))
        return {
            key: (spectrum[HALF * n : HALF * (n + 1), :128], spectrum[HALF * n : HALF * (n + 1), 128:])
            for n, key in enumerate(order)
        }

    def restore(g, spectra):
        size = HOLD * 3 * len(GROUPS[g])
        order = list(spectra)
        cos, sin = grid_ref[0], grid_ref[1]
        back = inner_step(
            back_ref, jnp.concatenate([jnp.concatenate(spectra[key], axis=1) for key in order], axis=0)
        )
        spun = []
        for n in range(len(order)):
            real, imag = back[HALF * n : HALF * (n + 1), :128], back[HALF * n : HALF * (n + 1), 128:]
            spun.append(jnp.concatenate([real * cos - imag * sin, imag * cos + real * sin], axis=0))
        cells = outer_step(last_ref[...], jnp.concatenate(spun, axis=1))
        for n, (row, pos) in enumerate(order):
            for s in range(3):
                snd[g][pl.ds(row * (size // HOLD) + 3 * pos + s, 32, stride=size), :] = cells[
                    32 * s : 32 * (s + 1), 128 * n : 128 * (n + 1)
                ]

    def put(ref, index, pair):
        ref[(*index, slice(0, HALF))] = pair[0]
        ref[(*index, slice(HALF, 2 * HALF))] = pair[1]

    def get(ref, *index):
        return ref[(*index, slice(0, HALF))], ref[(*index, slice(HALF, 2 * HALF))]

    row0 = jnp.where(south, NLAT - HOLD - HOLD * chain, HOLD * chain)

    def polar(row):
        steps = jnp.where(south, NLAT - 1 - row, row)
        return jnp.abs(jnp.full((1, 128), steps, jnp.int32).astype(F32) + 0.5) * (math.pi / NLAT)

    def cosine(w):
        return jnp.sin(polar(row0 + w - 1))

    def prepare():
        speed = speed_ref[0]
        share_of_pole = jnp.where(south, SPIN, -SPIN).astype(F32)
        for w in range(WINGS):
            there = 1.0
            if w == 0:
                there = jnp.where(has_before, 1.0, 0.0).astype(F32)
            if w == WINGS - 1:
                there = jnp.where(has_after, 1.0, 0.0).astype(F32)
            angle = polar(row0 + w - 1)
            share = 1.0 / jnp.maximum(grid_ref[3], jnp.sin(angle))
            keep = share * (jnp.sin(angle) * there)
            slope = share * (COURANT * grid_ref[2])
            scale[w, 0] = slope
            scale[w, 1] = keep * (share_of_pole * jnp.cos(angle))
            scale[w, 2] = keep * (0.5 * NORTH)
            if 0 < w < WINGS - 1:
                scale[w, 3] = speed * slope
                scale[w, 4] = share * (speed * (0.5 * NORTH) * cosine(w - 1))
                scale[w, 5] = share * (speed * (0.5 * NORTH) * cosine(w + 1))

    def push_winds(heights, old, new, w):
        low, mid, high = get(heights, w), get(heights, w + 1), get(heights, w + 2)
        east, north = get(old, w, 0), get(old, w, 1)
        slope, swirl, climb = scale[w, 0], scale[w, 1], scale[w, 2]
        put(new, (w, 0), (
            east[0] + slope * mid[1] + swirl * north[0],
            east[1] - slope * mid[0] + swirl * north[1],
        ))
        put(new, (w, 1), tuple(north[p] - climb * (high[p] - low[p]) - swirl * east[p] for p in range(2)))

    def pushed_height(heights, winds, w):
        mid, east = get(heights, w + 1), get(winds, w, 0)
        low, high = get(winds, w - 1, 1), get(winds, w + 1, 1)
        slope, below, above = scale[w, 3], scale[w, 4], scale[w, 5]
        return (
            mid[0] + slope * east[1] - (above * high[0] - below * low[0]),
            mid[1] - slope * east[0] - (above * high[1] - below * low[1]),
        )

    def trade(e, ref, wing):
        @pl.when(has_before)
        def _():
            remote(
                ref.at[pl.ds(wing, wing)], ref.at[pl.ds(wing + HOLD, wing)],
                send_x.at[e, 0], recv_x.at[e, 1], before_device,
            )

        @pl.when(has_after)
        def _():
            remote(ref.at[pl.ds(HOLD, wing)], ref.at[pl.ds(0, wing)], send_x.at[e, 1], recv_x.at[e, 0], after_device)

    def traded(e, ref, wing):
        pl.when(has_before)(lambda: landed(ref.at[pl.ds(0, wing)], recv_x.at[e, 0]))
        pl.when(has_after)(lambda: landed(ref.at[pl.ds(wing + HOLD, wing)], recv_x.at[e, 1]))

    def send_back(g):
        size = HOLD * 3 * len(GROUPS[g])
        start = first_row(chain - 32 * my_band) * (size // HOLD)

        def one(k, carry):
            to = lax.rem(chain + k, 32)
            send(
                snd[g].at[pl.ds(to * size, size)], ret[g].at[pl.ds(start, size)],
                send_c.at[g], recv_c.at[g], (my_lat, to),
            )
            return carry

        lax.fori_loop(0, 32, one, 0)

    @pl.when(owner)
    def _():
        loaded(3, 4, 5, 6, 7)
        prepare()

        @pl.when(jnp.logical_not(has_before))
        def _():
            tall[0:2] = jnp.zeros((2, 2 * HALF, 128), F32)
            tall_new[0:2] = jnp.zeros((2, 2 * HALF, 128), F32)
            wind[0] = jnp.zeros((2, 2 * HALF, 128), F32)

        @pl.when(jnp.logical_not(has_after))
        def _():
            tall[2 + HOLD : 4 + HOLD] = jnp.zeros((2, 2 * HALF, 128), F32)
            tall_new[2 + HOLD : 4 + HOLD] = jnp.zeros((2, 2 * HALF, 128), F32)
            wind[1 + HOLD] = jnp.zeros((2, 2 * HALF, 128), F32)

        landed(recv[0], recv_a.at[0])
        for (row, _), pair in transform(0).items():
            put(tall, (2 + row,), pair)
        trade(0, tall, 2)
        landed(recv[1], recv_a.at[1])
        for (row, which), pair in transform(1).items():
            put(wind, (1 + row, which), pair)
        trade(1, wind, 1)
        traded(0, tall, 2)
        traded(1, wind, 1)
        for w in range(WINGS):
            push_winds(tall, wind, wind_new, w)
        for w in range(1, 1 + HOLD):
            put(tall_new, (1 + w,), pushed_height(tall, wind_new, w))
        trade(2, tall_new, 2)
        traded(2, tall_new, 2)
        for w in range(WINGS):
            push_winds(tall_new, wind_new, wind_last, w)
        restore(1, {(row, which): get(wind_last, 1 + row, which) for row in range(HOLD) for which in range(2)})
        send_back(1)
        restore(0, {(row, 0): pushed_height(tall_new, wind_last, 1 + row) for row in range(HOLD)})
        send_back(0)

    @pl.when(stencil)
    def _():
        @pl.when(lat > 2)
        def _():
            landed(ext.at[:, 0:8, :], recv_r.at[1])

        @pl.when(lat < 13)
        def _():
            landed(ext.at[:, 104:112, :], recv_r.at[0])

        row = lax.broadcasted_iota(jnp.int32, (ROWS + 16, 128), 0) + (ROWS * lat - 8)
        latitude = (row.astype(F32) + (0.5 - NLAT // 2)) * (math.pi / NLAT)
        wide_cos = jnp.concatenate([jnp.cos(latitude)] * 4, axis=1)
        spin = jnp.concatenate([SPIN * jnp.sin(latitude)] * 4, axis=1)
        inverse = 1.0 / wide_cos
        east_scale = (0.5 * COURANT) * inverse
        speed = speed_ref[0]

        def across(value):
            return pltpu.roll(value, 511, 1) - pltpu.roll(value, 1, 1)

        def along(value):
            return pltpu.roll(value, ROWS + 15, 0) - pltpu.roll(value, 1, 0)

        height, east, north = ext[0], ext[1], ext[2]
        for _step in range(2):
            east_inc = spin * north - east_scale * across(height)
            north_inc = (-0.5 * NORTH) * along(height) - spin * east
            east, north = east + east_inc, north + north_inc
            spread_out = east_scale * across(east) + (0.5 * NORTH) * inverse * along(north * wide_cos)
            height = height - speed * spread_out
        for out, value in zip(outs, (height, east, north)):
            out[0] = value[8 : 8 + ROWS, 0:CELLS]

    def back(f, s):
        g = 0 if f == 0 else 1
        return ret[g][pl.ds(3 * GROUPS[g].index(f) + s, ROWS, stride=3 * len(GROUPS[g])), :]

    @pl.when(band < 2)
    def _():
        for g in (1, 0):
            landed(ret[g], recv_c.at[g])
            for f in GROUPS[g]:
                for s in range(3):
                    outs[f][0, :, 128 * s : 128 * (s + 1)] = back(f, s)

    @pl.when(band == 2)
    def _():
        row = lax.broadcasted_iota(jnp.int32, (ROWS, 128), 0)
        from_pole = jnp.where(south, ROWS - 1 - row, row) + 2 * ROWS
        for g in (1, 0):
            landed(ret[g].at[pl.ds(0, 24 * HOLD * 3 * len(GROUPS[g]))], recv_c.at[g])
            for f in GROUPS[g]:
                for s in range(3):
                    lanes = slice(128 * s, 128 * (s + 1))
                    outs[f][0, :, lanes] = jnp.where(from_pole < FINAL, back(f, s), outs[f][0, :, lanes])

    for g in range(2):
        size = HOLD * 3 * len(GROUPS[g])
        for case, count in (
            (jnp.logical_and(band < 2, jnp.logical_not(own_rows)), 32), (jnp.logical_and(band < 2, own_rows), 31),
            (jnp.logical_and(band == 2, jnp.logical_not(own_rows)), 24), (jnp.logical_and(band == 2, own_rows), 23),
        ):
            pl.when(case)(lambda g=g, size=size, count=count: landed(src[g].at[pl.ds(0, count * size)], send_a.at[g]))
        for case, count in (
            (jnp.logical_and(owner, jnp.logical_not(own_rows)), 32), (jnp.logical_and(owner, own_rows), 31),
        ):
            pl.when(case)(lambda g=g, size=size, count=count: landed(snd[g].at[pl.ds(0, count * size)], send_c.at[g]))

    @pl.when(stencil)
    def _():
        for side in range(2):
            landed(packed.at[side], send_s.at[side])

        @pl.when(lat > 2)
        def _():
            landed(ext.at[:, 8:16, :], send_r.at[0])

        @pl.when(lat < 13)
        def _():
            landed(ext.at[:, 96:104, :], send_r.at[1])

    for e, (ref, wing) in enumerate(((tall, 2), (wind, 1), (tall_new, 2))):
        pl.when(has_before)(lambda e=e, ref=ref, wing=wing: landed(ref.at[pl.ds(0, wing)], send_x.at[e, 0]))
        pl.when(has_after)(lambda e=e, ref=ref, wing=wing: landed(ref.at[pl.ds(0, wing)], send_x.at[e, 1]))


def body(height, east_wind, north_wind, wave_speed_sq):
    constants = [np.asarray(table, np.float32) for table in tables()]
    block = jax.ShapeDtypeStruct((1, ROWS, CELLS), F32)
    pairs = []
    for rows in (ROWS, 32 * HOLD, 32 * HOLD, ROWS):
        pairs += [pltpu.VMEM((rows * 3 * len(group), 128), F32) for group in GROUPS]
    dma = pltpu.SemaphoreType.DMA
    return pl.pallas_call(
        kernel,
        out_shape=[block] * 3,
        in_specs=[pl.BlockSpec(memory_space=pltpu.SMEM)] + [pl.BlockSpec(memory_space=pl.ANY)] * 8,
        out_specs=[pl.BlockSpec(memory_space=pltpu.VMEM)] * 3,
        scratch_shapes=[
            *[pltpu.VMEM((1, ROWS, CELLS), F32)] * 3,
            *[pltpu.VMEM(table.shape, table.dtype) for table in constants],
            *pairs,
            *[pltpu.VMEM((HOLD + 4, 2 * HALF, 128), F32)] * 2,
            *[pltpu.VMEM((WINGS, 2, 2 * HALF, 128), F32)] * 3,
            pltpu.VMEM((WINGS, 6, HALF, 128), F32),
            pltpu.VMEM((2, ROWS, 128), F32),
            pltpu.VMEM((2, ROWS, 128), F32),
            pltpu.VMEM((3, ROWS + 16, 512), F32),
            dma((8,)), dma((2,)), dma((2,)), dma((2,)), dma((2,)),
            dma((3, 2)), dma((3, 2)), dma((2,)), dma((2,)), dma((2,)), dma((2,)),
        ],
        compiler_params=pltpu.CompilerParams(
            collective_id=0, has_side_effects=True, vmem_limit_bytes=60 * 1024 * 1024
        ),
        name="substeps",
    )(wave_speed_sq, height, east_wind, north_wind, *constants)


def solution(mesh):
    block = P(None, "lat", "lon")
    return jax.shard_map(
        lambda *args: tuple(body(*args)),
        mesh=mesh, in_specs=(block, block, block, P()), out_specs=(block, block, block), check_vma=False,
    )
```

time: 80.3 us -> 78.3 us (0.975)
  the two profiles are of different devices: /device:TPU:29 before, /device:TPU:1 now
where the time goes in v3:
time: 78.3 us; the launch traced here: 76.8 us
  Pallas kernels  72.2 us (92%)
  local copies, waits for them, and re-layouts  3.25 us (4%)
  between operations  1.3 us (2%)
    pallas_call x1, Pallas kernels, body(): pl.pallas_call(kernel, out_shape=[block] * 3, in_specs=[pl.BlockSpec(memo...  72.2 us
    unnamed x7, local copies, waits for them, and re-layouts  3.25 us

profile of v3, /device:TPU:1, one launch (start us, length us, event | category | flops | bytes accessed | tf_op | source)
XLA Modules:
  0.0 76.8 jit_solution(12843776782004714913)
XLA Ops:
  1.3 72.2 %substeps.1 = (f32[1,96,384]{2,1,0:T(8,128)}, f32[1,96,384]{2,1,0:T(8,128)}, f32[1,96,384]{2,1,0:T(8,128)}) custom-call(f32[1]{0:T(128)S(6)} %copy.15.speed_ref, f32[1,96,384]{2,1,0:T(8,128)} %h_hbm.1, f32[1,96,384]{2,1,0:T(8,128)} %u_hbm.1, f32[1,96,384]{2,1,0:T(8,128)} %v_hbm.1, f32[112,288]{1,0:T(8,128)} %constant.10.clone.first_hbm, ...), custom_call_target="tpu_custom_call" | custom-call | tf_op jit(solution)/shard_map/substeps/pallas_call | solution.py:528
  73.5 0.0 copy-start.1
  73.5 1.6 %copy.16 = f32[1,96,384]{2,1,0:T(8,128)} copy(f32[1,96,384]{2,1,0:T(8,128)} %get-tuple-element.6) | data formatting | bytes 294912
  75.1 0.0 copy-done.1
  75.1 0.0 copy-start
  75.1 0.7 copy.17
  75.8 0.3 copy-done
  76.1 0.7 copy.18
Async XLA Ops:
  73.5 1.6 %copy-start.1 = (f32[1,96,384]{2,1,0:T(8,128)S(1)}, f32[1,96,384]{2,1,0:T(8,128)}, u32[]{:S(2)}) copy-start(f32[1,96,384]{2,1,0:T(8,128)} %get-tuple-element.7) | copy-start | bytes 442372
  75.1 1.0 %copy-start = (f32[1,96,384]{2,1,0:T(8,128)S(1)}, f32[1,96,384]{2,1,0:T(8,128)}, u32[]{:S(2)}) copy-start(f32[1,96,384]{2,1,0:T(8,128)} %get-tuple-element.8) | copy-start | bytes 442372

commit v4 on v3

--- a/solution.py
+++ b/solution.py
@@ -16,8 +16,8 @@
 COURANT, SPIN = 0.45, 0.3
 NORTH = COURANT * 2.0 * NLAT / NLON
 FINAL = 260
-HOLD = 3
-OWNERS = 88
+HOLD = 2
+OWNERS = 132
 WINGS = HOLD + 2
 MESH = pl.DeviceIdType.MESH
 F32, BF16 = jnp.float32, jnp.bfloat16
@@ -85,14 +85,15 @@
     speed_ref, h_hbm, u_hbm, v_hbm, first_hbm, last_hbm, fore_hbm, back_hbm, grid_hbm,
     h_out, u_out, v_out,
     h_ref, u_ref, v_ref, first_ref, last_ref, fore_ref, back_ref, grid_ref,
-    src0, src1, recv0, recv1, snd0, snd1, ret0, ret1,
+    src0, src1, relay0, relay1, recv0, recv1, snd0, snd1, home0, home1, ret0, ret1,
     tall, tall_new, wind, wind_new, wind_last, scale, packed, sides, ext,
-    loads, send_a, recv_a, send_c, recv_c, send_x, recv_x, send_s, recv_s, send_r, recv_r,
+    loads, send_a, recv_a, send_b, recv_b, send_c, recv_c, send_d, recv_d, send_x, recv_x, send_s, recv_s, send_r, recv_r,
 ):
     fields, outs = (h_ref, u_ref, v_ref), (h_out, u_out, v_out)
     operands = (h_hbm, u_hbm, v_hbm, first_hbm, last_hbm, fore_hbm, back_hbm, grid_hbm)
     held = (h_ref, u_ref, v_ref, first_ref, last_ref, fore_ref, back_ref, grid_ref)
-    src, recv, snd, ret = (src0, src1), (recv0, recv1), (snd0, snd1), (ret0, ret1)
+    src, relay, recv = (src0, src1), (relay0, relay1), (recv0, recv1)
+    snd, home, ret = (snd0, snd1), (home0, home1), (ret0, ret1)
     lat, lon = lax.axis_index("lat"), lax.axis_index("lon")
     south = lat >= 8
     band = jnp.where(south, 15 - lat, lat)
@@ -100,21 +101,40 @@
     z = lax.rem(lon, 16)
     x = 2 * lax.div(lon, 16) + lax.rem(lax.div(band, 2), 2)
     line = jnp.where(band < 4, x, 7 - x)
-    step = lax.rem(z + line, 16) + jnp.where(lax.rem(z + line, 16) < lax.rem(10 * line + line, 16), 16, 0)
-    nth = step - lax.rem(11 * line, 16)
-    owner = jnp.logical_and(core == 1, nth < 11)
-    chain = 11 * line + nth
+    wide = line >= 6
+    near = lax.rem(z + line, 16)
+    slab = 16 * core + z
+    extra = jnp.logical_and(wide, jnp.logical_and(core == 0, jnp.logical_or(near == 0, near == 15)))
+    owner = jnp.logical_or(core == 1, extra)
+    owners = jnp.where(wide, 18, 16)
+    nth = jnp.where(wide, jnp.where(core == 1, near + 1, jnp.where(near == 0, 0, 17)), near)
+    chain = 16 * line + 2 * jnp.where(line == 7, 1, 0) + nth
     source = band <= 2
     stencil = band >= 2
-    partners = jnp.where(band < 2, 32, 24)
-    my_band = jnp.minimum(lax.div(chain, 32), 2)
+    my_band = jnp.where(wide, 2, lax.div(line, 3))
     my_lat = jnp.where(south, 15 - my_band, my_band)
+    my_part = line - 3 * my_band
+
+    def member(to_line, to_z, to_core):
+        to_x = jnp.where(to_line < 4, to_line, 7 - to_line)
+        to_band = 4 * lax.div(to_line, 4) + 2 * lax.rem(to_x, 2) + to_core
+        return jnp.where(south, 15 - to_band, to_band), 16 * lax.div(to_x, 2) + to_z
+
+    def mate(to_z, to_core):
+        shift = to_core - core
+        return jnp.where(south, lat - shift, lat + shift), lon - z + to_z
 
     def holder(n):
-        to_line = lax.div(n, 11)
-        to_x = jnp.where(to_line < 4, to_line, 7 - to_line)
-        to_band = 4 * lax.div(to_line, 4) + 2 * lax.rem(to_x, 2) + 1
-        return jnp.where(south, 15 - to_band, to_band), 16 * lax.div(to_x, 2) + lax.rem(n + 16 - to_line, 16)
+        to_line = jnp.where(n < 96, lax.div(n, 16), 6 + lax.div(jnp.maximum(n - 96, 0), 18))
+        to_nth = n - 16 * to_line - 2 * jnp.where(to_line == 7, 1, 0)
+        broad = to_line >= 6
+        to_near = jnp.where(broad, jnp.clip(to_nth - 1, 0, 15), to_nth)
+        to_core = jnp.where(jnp.logical_and(broad, jnp.logical_or(to_nth == 0, to_nth == 17)), 0, 1)
+        return member(to_line, lax.rem(to_near + 16 - to_line, 16), to_core)
+
+    def chip(k):
+        away = 8 - lax.div(k + 1, 2)
+        return lax.rem(z + 16 + jnp.where(lax.rem(k, 2) == 1, away, -away), 16)
 
     def same(target):
         return jnp.logical_and(target[0] == lat, target[1] == lon)
@@ -138,8 +158,15 @@
     def landed(ref, sem):
         pltpu.make_async_copy(ref, ref, sem).wait()
 
-    def first_row(i):
-        return jnp.where(south, ROWS - HOLD - HOLD * i, HOLD * i)
+    def part_start(k, size):
+        return jnp.where(south, ROWS - size * (k + 1), size * k)
+
+    def owner_start(i):
+        return HOLD * jnp.where(south, owners - 1 - i, i)
+
+    def each_size(act):
+        pl.when(jnp.logical_not(wide))(lambda: act(32))
+        pl.when(wide)(lambda: act(36))
 
     right = jnp.where(lon == 31, 0, lon + 1)
     left = jnp.where(lon == 0, 31, lon - 1)
@@ -147,7 +174,7 @@
     after = chain + jnp.where(south, -1, 1)
     has_before = jnp.logical_and(owner, jnp.logical_and(before >= 0, before < OWNERS))
     has_after = jnp.logical_and(owner, jnp.logical_and(after >= 0, after < OWNERS))
-    before_device, after_device = holder(jnp.maximum(before, 0)), holder(jnp.maximum(after, 0))
+    before_device, after_device = holder(jnp.clip(before, 0, OWNERS - 1)), holder(jnp.clip(after, 0, OWNERS - 1))
 
     barrier = pltpu.get_barrier_semaphore()
 
@@ -157,27 +184,31 @@
     def greet_other(target):
         pl.when(jnp.logical_not(same(target)))(lambda: greet(target))
 
-    def target_of(k):
-        return lax.rem(lon + k, partners)
-
-    def greet_holder(k, carry):
-        greet_other(holder(32 * band + k))
+    def greet_chip(k, carry):
+        to = lax.rem(z + k, 16)
+        greet(mate(to, 1))
+        pl.when(owner)(lambda: greet(mate(to, 0)))
         return carry
 
-    def greet_source(k, carry):
-        greet_other((my_lat, k))
-        return carry
-
-    @pl.when(owner)
-    def _():
-        lax.fori_loop(0, 32, greet_source, 0)
-
-    @pl.when(source)
-    def _():
-        lax.fori_loop(0, partners, greet_holder, 0)
-
-    own_rows = jnp.logical_and(jnp.logical_and(owner, source), my_band == band)
-    greeted = jnp.where(owner, 32, 0) + jnp.where(source, partners, 0) - jnp.where(own_rows, 2, 0)
+    lax.fori_loop(1, 16, greet_chip, 0)
+    greeted = jnp.where(owner, 30, 15)
+    own_chip = jnp.logical_or(core == 0, owner)
+    pl.when(own_chip)(lambda: greet(mate(z, 1 - core)))
+    greeted += own_chip.astype(jnp.int32)
+    for end in (0, 15):
+        there = lax.rem(end + 16 - line, 16)
+        meant = jnp.logical_and(wide, jnp.logical_not(jnp.logical_or(owner, there == z)))
+        pl.when(meant)(lambda there=there: greet(mate(there, 0)))
+        greeted += meant.astype(jnp.int32)
+    meant = jnp.logical_not(same((my_lat, slab)))
+    pl.when(meant)(lambda: greet((my_lat, slab)))
+    greeted += meant.astype(jnp.int32)
+    for k in range(3):
+        target = member(jnp.minimum(3 * band + k, 7), z, lax.div(lon, 16))
+        meant = jnp.logical_or(band < 2, jnp.logical_and(band == 2, k < 2))
+        meant = jnp.logical_and(meant, jnp.logical_not(same(target)))
+        pl.when(meant)(lambda target=target: greet(target))
+        greeted += meant.astype(jnp.int32)
     for meant, target in (
         (has_before, before_device), (has_after, after_device), (stencil, (lat, left)), (stencil, (lat, right)),
         (jnp.logical_and(stencil, lat > 2), (lat - 1, lon)), (jnp.logical_and(stencil, lat < 13), (lat + 1, lon)),
@@ -203,17 +234,23 @@
                 src[g][pl.ds(3 * pos + s, ROWS, stride=per), :] = fields[f][0, :, 128 * s : 128 * (s + 1)]
 
     def send_rows(g):
-        size = HOLD * 3 * len(GROUPS[g])
-
-        def one(k, carry):
-            i = target_of(k)
+        per = 3 * len(GROUPS[g])
+
+        def one(k, size):
             send(
-                src[g].at[pl.ds(first_row(i) * (size // HOLD), size)], recv[g].at[pl.ds(lon * size, size)],
-                send_a.at[g], recv_a.at[g], holder(32 * band + i),
+                src[g].at[pl.ds(part_start(k, size) * per, size * per)], relay[g].at[pl.ds(0, size * per)],
+                send_a.at[g, k], recv_a.at[g], member(3 * band + k, z, lax.div(lon, 16)),
             )
-            return carry
-
-        lax.fori_loop(0, partners, one, 0)
+
+        @pl.when(band < 2)
+        def _():
+            for k in range(3):
+                one(k, 32)
+
+        @pl.when(band == 2)
+        def _():
+            for k in range(2):
+                one(k, 36)
 
     loaded(0)
     pl.when(source)(lambda: gather(0))
@@ -237,6 +274,30 @@
         packed[1] = jnp.where(lane < 4, low[0], jnp.where(lane < 8, pltpu.roll(low[1], 4, 1), pltpu.roll(low[2], 8, 1)))
         remote(packed.at[0], sides.at[0], send_s.at[0], recv_s.at[0], (lat, right))
         remote(packed.at[1], sides.at[1], send_s.at[1], recv_s.at[1], (lat, left))
+
+    for g in range(2):
+        per = 3 * len(GROUPS[g])
+        each_size(lambda size, g=g, per=per: landed(relay[g].at[pl.ds(0, size * per)], recv_a.at[g]))
+
+        def to_owner(how, i, target, g=g, per=per):
+            how(
+                relay[g].at[pl.ds(owner_start(i) * per, HOLD * per)],
+                recv[g].at[pl.ds(slab * (HOLD * per), HOLD * per)],
+                send_b.at[g], recv_b.at[g], target,
+            )
+
+        def spread(k, carry, to_owner=to_owner):
+            to = chip(k)
+            to_owner(remote, lax.rem(to + line, 16) + jnp.where(wide, 1, 0), mate(to, 1))
+            return carry
+
+        @pl.when(wide)
+        def _(to_owner=to_owner):
+            for i in (0, 17):
+                to_owner(send, i, mate(lax.rem(min(i, 15) + 16 - line, 16), 0))
+
+        lax.fori_loop(0, 15, spread, 0)
+        to_owner(send, near + jnp.where(wide, 1, 0), mate(z, 1))
 
     @pl.when(stencil)
     def _():
@@ -379,17 +440,23 @@
 
     def send_back(g):
         size = HOLD * 3 * len(GROUPS[g])
-        start = first_row(chain - 32 * my_band) * (size // HOLD)
-
-        def one(k, carry):
-            to = lax.rem(chain + k, 32)
-            send(
-                snd[g].at[pl.ds(to * size, size)], ret[g].at[pl.ds(start, size)],
-                send_c.at[g], recv_c.at[g], (my_lat, to),
+        start = owner_start(nth) * (size // HOLD)
+
+        def one(how, to_z, to_core):
+            how(
+                snd[g].at[pl.ds((16 * to_core + to_z) * size, size)], home[g].at[pl.ds(start, size)],
+                send_c.at[g], recv_c.at[g], mate(to_z, to_core),
             )
+
+        def both(k, carry):
+            to = chip(k)
+            one(remote, to, 0)
+            one(remote, to, 1)
             return carry
 
-        lax.fori_loop(0, 32, one, 0)
+        lax.fori_loop(0, 15, both, 0)
+        one(send, z, 0)
+        one(send, z, 1)
 
     @pl.when(owner)
     def _():
@@ -408,11 +475,11 @@
             tall_new[2 + HOLD : 4 + HOLD] = jnp.zeros((2, 2 * HALF, 128), F32)
             wind[1 + HOLD] = jnp.zeros((2, 2 * HALF, 128), F32)
 
-        landed(recv[0], recv_a.at[0])
+        landed(recv[0], recv_b.at[0])
         for (row, _), pair in transform(0).items():
             put(tall, (2 + row,), pair)
         trade(0, tall, 2)
-        landed(recv[1], recv_a.at[1])
+        landed(recv[1], recv_b.at[1])
         for (row, which), pair in transform(1).items():
             put(wind, (1 + row, which), pair)
         trade(1, wind, 1)
@@ -431,6 +498,18 @@
         restore(0, {(row, 0): pushed_height(tall_new, wind_last, 1 + row) for row in range(HOLD)})
         send_back(0)
 
+    for g in (1, 0):
+        per = 3 * len(GROUPS[g])
+
+        def deliver(size, g=g, per=per):
+            landed(home[g].at[pl.ds(0, size * per)], recv_c.at[g])
+            send(
+                home[g].at[pl.ds(0, size * per)], ret[g].at[pl.ds(part_start(my_part, size) * per, size * per)],
+                send_d.at[g], recv_d.at[g, my_part], (my_lat, slab),
+            )
+
+        each_size(deliver)
+
     @pl.when(stencil)
     def _():
         @pl.when(lat > 2)
@@ -472,7 +551,9 @@
     @pl.when(band < 2)
     def _():
         for g in (1, 0):
-            landed(ret[g], recv_c.at[g])
+            per = 3 * len(GROUPS[g])
+            for k in range(3):
+                landed(ret[g].at[pl.ds(part_start(k, 32) * per, 32 * per)], recv_d.at[g, k])
             for f in GROUPS[g]:
                 for s in range(3):
                     outs[f][0, :, 128 * s : 128 * (s + 1)] = back(f, s)
@@ -482,23 +563,38 @@
         row = lax.broadcasted_iota(jnp.int32, (ROWS, 128), 0)
         from_pole = jnp.where(south, ROWS - 1 - row, row) + 2 * ROWS
         for g in (1, 0):
-            landed(ret[g].at[pl.ds(0, 24 * HOLD * 3 * len(GROUPS[g]))], recv_c.at[g])
+            per = 3 * len(GROUPS[g])
+            for k in range(2):
+                landed(ret[g].at[pl.ds(part_start(k, 36) * per, 36 * per)], recv_d.at[g, k])
             for f in GROUPS[g]:
                 for s in range(3):
                     lanes = slice(128 * s, 128 * (s + 1))
                     outs[f][0, :, lanes] = jnp.where(from_pole < FINAL, back(f, s), outs[f][0, :, lanes])
 
     for g in range(2):
-        size = HOLD * 3 * len(GROUPS[g])
+        per = 3 * len(GROUPS[g])
+
+        def left_parts(size, parts, g=g, per=per):
+            for k in range(parts):
+                other = jnp.logical_not(same(member(3 * band + k, z, lax.div(lon, 16))))
+                pl.when(other)(lambda k=k: landed(src[g].at[pl.ds(0, size * per)], send_a.at[g, k]))
+
+        pl.when(band < 2)(lambda f=left_parts: f(32, 3))
+        pl.when(band == 2)(lambda f=left_parts: f(36, 2))
         for case, count in (
-            (jnp.logical_and(band < 2, jnp.logical_not(own_rows)), 32), (jnp.logical_and(band < 2, own_rows), 31),
-            (jnp.logical_and(band == 2, jnp.logical_not(own_rows)), 24), (jnp.logical_and(band == 2, own_rows), 23),
+            (jnp.logical_and(jnp.logical_not(wide), owner), 15),
+            (jnp.logical_and(jnp.logical_not(wide), jnp.logical_not(owner)), 16),
+            (jnp.logical_and(wide, owner), 17),
+            (jnp.logical_and(wide, jnp.logical_not(owner)), 18),
         ):
-            pl.when(case)(lambda g=g, size=size, count=count: landed(src[g].at[pl.ds(0, count * size)], send_a.at[g]))
-        for case, count in (
-            (jnp.logical_and(owner, jnp.logical_not(own_rows)), 32), (jnp.logical_and(owner, own_rows), 31),
-        ):
-            pl.when(case)(lambda g=g, size=size, count=count: landed(snd[g].at[pl.ds(0, count * size)], send_c.at[g]))
+            pl.when(case)(
+                lambda g=g, n=count * HOLD * per: landed(relay[g].at[pl.ds(0, n)], send_b.at[g])
+            )
+        pl.when(owner)(lambda g=g, per=per: landed(snd[g].at[pl.ds(0, 31 * HOLD * per)], send_c.at[g]))
+
+        @pl.when(jnp.logical_not(same((my_lat, slab))))
+        def _(g=g, per=per):
+            each_size(lambda size: landed(home[g].at[pl.ds(0, size * per)], send_d.at[g]))
 
     @pl.when(stencil)
     def _():
@@ -522,7 +618,7 @@
     constants = [np.asarray(table, np.float32) for table in tables()]
     block = jax.ShapeDtypeStruct((1, ROWS, CELLS), F32)
     pairs = []
-    for rows in (ROWS, 32 * HOLD, 32 * HOLD, ROWS):
+    for rows in (ROWS, 36, 32 * HOLD, 32 * HOLD, 36, ROWS):
         pairs += [pltpu.VMEM((rows * 3 * len(group), 128), F32) for group in GROUPS]
     dma = pltpu.SemaphoreType.DMA
     return pl.pallas_call(
@@ -540,7 +636,7 @@
             pltpu.VMEM((2, ROWS, 128), F32),
             pltpu.VMEM((2, ROWS, 128), F32),
             pltpu.VMEM((3, ROWS + 16, 512), F32),
-            dma((8,)), dma((2,)), dma((2,)), dma((2,)), dma((2,)),
+            dma((8,)), dma((2, 3)), dma((2,)), dma((2,)), dma((2,)), dma((2,)), dma((2,)), dma((2,)), dma((2, 3)),
             dma((3, 2)), dma((3, 2)), dma((2,)), dma((2,)), dma((2,)), dma((2,)),
         ],
         compiler_params=pltpu.CompilerParams(

time: 78.3 us -> 61.4 us (0.78)
  the two profiles are of different devices: /device:TPU:1 before, /device:TPU:6 now
where the time goes in v4:
time: 61.4 us; the launch traced here: 61.2 us
  Pallas kernels  56.6 us (92%)
  local copies, waits for them, and re-layouts  3.25 us (5%)
  between operations  1.3 us (2%)
    pallas_call x1, Pallas kernels, body(): pl.pallas_call(kernel, out_shape=[block] * 3, in_specs=[pl.BlockSpec(memo...  56.6 us
    unnamed x7, local copies, waits for them, and re-layouts  3.25 us

profile of v4, /device:TPU:6, one launch (start us, length us, event | category | flops | bytes accessed | tf_op | source)
XLA Modules:
  0.0 61.2 jit_solution(6195930926897262868)
XLA Ops:
  1.3 56.6 %substeps.1 = (f32[1,96,384]{2,1,0:T(8,128)}, f32[1,96,384]{2,1,0:T(8,128)}, f32[1,96,384]{2,1,0:T(8,128)}) custom-call(f32[1]{0:T(128)S(6)} %copy.15.speed_ref, f32[1,96,384]{2,1,0:T(8,128)} %h_hbm.1, f32[1,96,384]{2,1,0:T(8,128)} %u_hbm.1, f32[1,96,384]{2,1,0:T(8,128)} %v_hbm.1, f32[112,288]{1,0:T(8,128)} %constant.10.clone.first_hbm, ...), custom_call_target="tpu_custom_call" | custom-call | tf_op jit(solution)/shard_map/substeps/pallas_call | solution.py:624
  57.9 0.0 copy-start.1
  57.9 1.6 %copy.16 = f32[1,96,384]{2,1,0:T(8,128)} copy(f32[1,96,384]{2,1,0:T(8,128)} %get-tuple-element.6) | data formatting | bytes 294912
  59.6 0.0 copy-done.1
  59.6 0.0 copy-start
  59.6 0.7 %copy.17 = f32[1,96,384]{2,1,0:T(8,128)} copy(f32[1,96,384]{2,1,0:T(8,128)S(1)} %copy-done.1) | data formatting | bytes 294912
  60.2 0.3 copy-done
  60.5 0.7 %copy.18 = f32[1,96,384]{2,1,0:T(8,128)} copy(f32[1,96,384]{2,1,0:T(8,128)S(1)} %copy-done) | data formatting | bytes 294912
Async XLA Ops:
  57.9 1.6 %copy-start.1 = (f32[1,96,384]{2,1,0:T(8,128)S(1)}, f32[1,96,384]{2,1,0:T(8,128)}, u32[]{:S(2)}) copy-start(f32[1,96,384]{2,1,0:T(8,128)} %get-tuple-element.7) | copy-start | bytes 442372
  59.6 1.0 %copy-start = (f32[1,96,384]{2,1,0:T(8,128)S(1)}, f32[1,96,384]{2,1,0:T(8,128)}, u32[]{:S(2)}) copy-start(f32[1,96,384]{2,1,0:T(8,128)} %get-tuple-element.8) | copy-start | bytes 442372

commit v5 on v4

--- a/solution.py
+++ b/solution.py
@@ -22,6 +22,7 @@
 MESH = pl.DeviceIdType.MESH
 F32, BF16 = jnp.float32, jnp.bfloat16
 GROUPS = ((0,), (1, 2))
+BACK = ((1,), (2, 0))
 
 
 def split(table):
@@ -349,7 +350,7 @@
         }
 
     def restore(g, spectra):
-        size = HOLD * 3 * len(GROUPS[g])
+        size = HOLD * 3 * len(BACK[g])
         order = list(spectra)
         cos, sin = grid_ref[0], grid_ref[1]
         back = inner_step(
@@ -403,14 +404,18 @@
                 scale[w, 4] = share * (speed * (0.5 * NORTH) * cosine(w - 1))
                 scale[w, 5] = share * (speed * (0.5 * NORTH) * cosine(w + 1))
 
-    def push_winds(heights, old, new, w):
-        low, mid, high = get(heights, w), get(heights, w + 1), get(heights, w + 2)
-        east, north = get(old, w, 0), get(old, w, 1)
-        slope, swirl, climb = scale[w, 0], scale[w, 1], scale[w, 2]
+    def push_east(heights, old, new, w):
+        mid, east, north = get(heights, w + 1), get(old, w, 0), get(old, w, 1)
+        slope, swirl = scale[w, 0], scale[w, 1]
         put(new, (w, 0), (
             east[0] + slope * mid[1] + swirl * north[0],
             east[1] - slope * mid[0] + swirl * north[1],
         ))
+
+    def push_north(heights, old, new, w):
+        low, high = get(heights, w), get(heights, w + 2)
+        east, north = get(old, w, 0), get(old, w, 1)
+        swirl, climb = scale[w, 1], scale[w, 2]
         put(new, (w, 1), tuple(north[p] - climb * (high[p] - low[p]) - swirl * east[p] for p in range(2)))
 
     def pushed_height(heights, winds, w):
@@ -439,7 +444,7 @@
         pl.when(has_after)(lambda: landed(ref.at[pl.ds(wing + HOLD, wing)], recv_x.at[e, 1]))
 
     def send_back(g):
-        size = HOLD * 3 * len(GROUPS[g])
+        size = HOLD * 3 * len(BACK[g])
         start = owner_start(nth) * (size // HOLD)
 
         def one(how, to_z, to_core):
@@ -486,20 +491,25 @@
         traded(0, tall, 2)
         traded(1, wind, 1)
         for w in range(WINGS):
-            push_winds(tall, wind, wind_new, w)
+            push_east(tall, wind, wind_new, w)
+            push_north(tall, wind, wind_new, w)
         for w in range(1, 1 + HOLD):
             put(tall_new, (1 + w,), pushed_height(tall, wind_new, w))
         trade(2, tall_new, 2)
+        for w in range(1, 1 + HOLD):
+            push_east(tall_new, wind_new, wind_last, w)
+        restore(0, {(row, 0): get(wind_last, 1 + row, 0) for row in range(HOLD)})
+        send_back(0)
         traded(2, tall_new, 2)
         for w in range(WINGS):
-            push_winds(tall_new, wind_new, wind_last, w)
-        restore(1, {(row, which): get(wind_last, 1 + row, which) for row in range(HOLD) for which in range(2)})
+            push_north(tall_new, wind_new, wind_last, w)
+        last = {(row, 0): get(wind_last, 1 + row, 1) for row in range(HOLD)}
+        last.update({(row, 1): pushed_height(tall_new, wind_last, 1 + row) for row in range(HOLD)})
+        restore(1, last)
         send_back(1)
-        restore(0, {(row, 0): pushed_height(tall_new, wind_last, 1 + row) for row in range(HOLD)})
-        send_back(0)
-
-    for g in (1, 0):
-        per = 3 * len(GROUPS[g])
+
+    for g in range(2):
+        per = 3 * len(BACK[g])
 
         def deliver(size, g=g, per=per):
             landed(home[g].at[pl.ds(0, size * per)], recv_c.at[g])
@@ -545,16 +555,16 @@
             out[0] = value[8 : 8 + ROWS, 0:CELLS]
 
     def back(f, s):
-        g = 0 if f == 0 else 1
-        return ret[g][pl.ds(3 * GROUPS[g].index(f) + s, ROWS, stride=3 * len(GROUPS[g])), :]
+        g = 0 if f in BACK[0] else 1
+        return ret[g][pl.ds(3 * BACK[g].index(f) + s, ROWS, stride=3 * len(BACK[g])), :]
 
     @pl.when(band < 2)
     def _():
-        for g in (1, 0):
-            per = 3 * len(GROUPS[g])
+        for g in range(2):
+            per = 3 * len(BACK[g])
             for k in range(3):
                 landed(ret[g].at[pl.ds(part_start(k, 32) * per, 32 * per)], recv_d.at[g, k])
-            for f in GROUPS[g]:
+            for f in BACK[g]:
                 for s in range(3):
                     outs[f][0, :, 128 * s : 128 * (s + 1)] = back(f, s)
 
@@ -562,11 +572,11 @@
     def _():
         row = lax.broadcasted_iota(jnp.int32, (ROWS, 128), 0)
         from_pole = jnp.where(south, ROWS - 1 - row, row) + 2 * ROWS
-        for g in (1, 0):
-            per = 3 * len(GROUPS[g])
+        for g in range(2):
+            per = 3 * len(BACK[g])
             for k in range(2):
                 landed(ret[g].at[pl.ds(part_start(k, 36) * per, 36 * per)], recv_d.at[g, k])
-            for f in GROUPS[g]:
+            for f in BACK[g]:
                 for s in range(3):
                     lanes = slice(128 * s, 128 * (s + 1))
                     outs[f][0, :, lanes] = jnp.where(from_pole < FINAL, back(f, s), outs[f][0, :, lanes])
@@ -590,10 +600,11 @@
             pl.when(case)(
                 lambda g=g, n=count * HOLD * per: landed(relay[g].at[pl.ds(0, n)], send_b.at[g])
             )
-        pl.when(owner)(lambda g=g, per=per: landed(snd[g].at[pl.ds(0, 31 * HOLD * per)], send_c.at[g]))
+        ret_per = 3 * len(BACK[g])
+        pl.when(owner)(lambda g=g, per=ret_per: landed(snd[g].at[pl.ds(0, 31 * HOLD * per)], send_c.at[g]))
 
         @pl.when(jnp.logical_not(same((my_lat, slab))))
-        def _(g=g, per=per):
+        def _(g=g, per=ret_per):
             each_size(lambda size: landed(home[g].at[pl.ds(0, size * per)], send_d.at[g]))
 
     @pl.when(stencil)
@@ -612,20 +623,32 @@
     for e, (ref, wing) in enumerate(((tall, 2), (wind, 1), (tall_new, 2))):
         pl.when(has_before)(lambda e=e, ref=ref, wing=wing: landed(ref.at[pl.ds(0, wing)], send_x.at[e, 0]))
         pl.when(has_after)(lambda e=e, ref=ref, wing=wing: landed(ref.at[pl.ds(0, wing)], send_x.at[e, 1]))
+
+
+def write(h_ref, u_ref, v_ref, h_out, u_out, v_out, sems):
+    copies = [
+        pltpu.make_async_copy(here, there, sems.at[n])
+        for n, (here, there) in enumerate(((h_ref, h_out), (u_ref, u_out), (v_ref, v_out)))
+    ]
+    for copy in copies:
+        copy.start()
+    for copy in copies:
+        copy.wait()
 
 
 def body(height, east_wind, north_wind, wave_speed_sq):
     constants = [np.asarray(table, np.float32) for table in tables()]
     block = jax.ShapeDtypeStruct((1, ROWS, CELLS), F32)
     pairs = []
-    for rows in (ROWS, 36, 32 * HOLD, 32 * HOLD, 36, ROWS):
-        pairs += [pltpu.VMEM((rows * 3 * len(group), 128), F32) for group in GROUPS]
+    for groups, rows in ((GROUPS, ROWS), (GROUPS, 36), (GROUPS, 32 * HOLD), (BACK, 32 * HOLD), (BACK, 36), (BACK, ROWS)):
+        pairs += [pltpu.VMEM((rows * 3 * len(group), 128), F32) for group in groups]
     dma = pltpu.SemaphoreType.DMA
-    return pl.pallas_call(
+    vmem = pl.BlockSpec(memory_space=pltpu.VMEM)
+    results = pl.pallas_call(
         kernel,
-        out_shape=[block] * 3,
+        out_shape=[pltpu.VMEM(block.shape, F32)] * 3,
         in_specs=[pl.BlockSpec(memory_space=pltpu.SMEM)] + [pl.BlockSpec(memory_space=pl.ANY)] * 8,
-        out_specs=[pl.BlockSpec(memory_space=pltpu.VMEM)] * 3,
+        out_specs=[vmem] * 3,
         scratch_shapes=[
             *[pltpu.VMEM((1, ROWS, CELLS), F32)] * 3,
             *[pltpu.VMEM(table.shape, table.dtype) for table in constants],
@@ -644,6 +667,15 @@
         ),
         name="substeps",
     )(wave_speed_sq, height, east_wind, north_wind, *constants)
+    return pl.pallas_call(
+        write,
+        out_shape=[block] * 3,
+        in_specs=[vmem] * 3,
+        out_specs=[pl.BlockSpec(memory_space=pl.ANY)] * 3,
+        scratch_shapes=[dma((3,))],
+        compiler_params=pltpu.CompilerParams(vmem_limit_bytes=16 * 1024 * 1024),
+        name="write",
+    )(*results)
 
 
 def solution(mesh):

time: 61.4 us -> 56.4 us (0.919)
  the two profiles are of different devices: /device:TPU:6 before, /device:TPU:1 now
where the time goes in v5:
time: 56.4 us; the launch traced here: 55.5 us
  Pallas kernels  54.2 us (96%)
  between operations  1.29 us (2%)
    pallas_call x1, Pallas kernels, body(): pl.pallas_call(kernel, out_shape=[pltpu.VMEM(block.shape, F32)] * 3, in_s...  53.4 us

profile of v5, /device:TPU:1, one launch (start us, length us, event | category | flops | bytes accessed | tf_op | source)
XLA Modules:
  0.0 55.5 jit_solution(17182800374060406020)
XLA Ops:
  1.3 53.4 %substeps.1 = (f32[1,96,384]{2,1,0:T(8,128)S(1)}, f32[1,96,384]{2,1,0:T(8,128)S(1)}, f32[1,96,384]{2,1,0:T(8,128)S(1)}) custom-call(f32[1]{0:T(128)S(6)} %copy.12.speed_ref, f32[1,96,384]{2,1,0:T(8,128)} %h_hbm.1, f32[1,96,384]{2,1,0:T(8,128)} %u_hbm.1, f32[1,96,384]{2,1,0:T(8,128)} %v_hbm.1, f32[112,288]{1,0:T(8,128)} %constant.10.clone.first_hbm, ...), custom_call_target="tpu_custom_call" | custom-call | tf_op jit(solution)/shard_map/substeps/pallas_call | solution.py:647
  54.7 0.8 %write.1 = (f32[1,96,384]{2,1,0:T(8,128)}, f32[1,96,384]{2,1,0:T(8,128)}, f32[1,96,384]{2,1,0:T(8,128)}) custom-call(f32[1,96,384]{2,1,0:T(8,128)S(1)} %get-tuple-element.6.h_ref, f32[1,96,384]{2,1,0:T(8,128)S(1)} %get-tuple-element.7.u_ref, f32[1,96,384]{2,1,0:T(8,128)S(1)} %get-tuple-element.8.v_ref), custom_call_target="tpu_custom_call" | custom-call | tf_op jit(solution)/shard_map/write/pallas_call | solution.py:670

commit v6 on v5

--- a/solution.py
+++ b/solution.py
@@ -88,7 +88,7 @@
     h_ref, u_ref, v_ref, first_ref, last_ref, fore_ref, back_ref, grid_ref,
     src0, src1, relay0, relay1, recv0, recv1, snd0, snd1, home0, home1, ret0, ret1,
     tall, tall_new, wind, wind_new, wind_last, scale, packed, sides, ext,
-    loads, send_a, recv_a, send_b, recv_b, send_c, recv_c, send_d, recv_d, send_x, recv_x, send_s, recv_s, send_r, recv_r,
+    go, loads, send_a, recv_a, send_b, recv_b, send_c, recv_c, send_d, recv_d, send_x, recv_x, send_s, recv_s, send_r, recv_r,
 ):
     fields, outs = (h_ref, u_ref, v_ref), (h_out, u_out, v_out)
     operands = (h_hbm, u_hbm, v_hbm, first_hbm, last_hbm, fore_hbm, back_hbm, grid_hbm)
@@ -185,30 +185,32 @@
     def greet_other(target):
         pl.when(jnp.logical_not(same(target)))(lambda: greet(target))
 
-    def greet_chip(k, carry):
-        to = lax.rem(z + k, 16)
-        greet(mate(to, 1))
-        pl.when(owner)(lambda: greet(mate(to, 0)))
+    def helper(of_line, to_z):
+        of_x = jnp.where(of_line < 4, of_line, 7 - of_line)
+        return member(7 - of_x, to_z, lax.div(of_line, 4))
+
+    helps = band >= 4
+    helped = jnp.where(core == 1, 7 - x, x)
+
+    def greet_helper(k, carry):
+        greet(helper(line, lax.rem(z + k, 16)))
         return carry
 
-    lax.fori_loop(1, 16, greet_chip, 0)
-    greeted = jnp.where(owner, 30, 15)
-    own_chip = jnp.logical_or(core == 0, owner)
-    pl.when(own_chip)(lambda: greet(mate(z, 1 - core)))
-    greeted += own_chip.astype(jnp.int32)
-    for end in (0, 15):
-        there = lax.rem(end + 16 - line, 16)
-        meant = jnp.logical_and(wide, jnp.logical_not(jnp.logical_or(owner, there == z)))
-        pl.when(meant)(lambda there=there: greet(mate(there, 0)))
-        greeted += meant.astype(jnp.int32)
-    meant = jnp.logical_not(same((my_lat, slab)))
-    pl.when(meant)(lambda: greet((my_lat, slab)))
-    greeted += meant.astype(jnp.int32)
+    my_helper = helper(line, z)
+    helped_from_afar = jnp.logical_not(same(my_helper))
+
+    @pl.when(owner)
+    def _():
+        lax.fori_loop(1, 16, greet_helper, 0)
+
+    pl.when(jnp.logical_and(owner, helped_from_afar))(lambda: greet(my_helper))
+    pl.when(helped_from_afar)(lambda: greet(my_helper))
+    greeted = jnp.where(helps, jnp.where(helped >= 6, 18, 16) + 2 - 2 * core, 0)
+    pl.when(jnp.logical_not(same((my_lat, slab))))(lambda: greet((my_lat, slab)))
     for k in range(3):
         target = member(jnp.minimum(3 * band + k, 7), z, lax.div(lon, 16))
         meant = jnp.logical_or(band < 2, jnp.logical_and(band == 2, k < 2))
         meant = jnp.logical_and(meant, jnp.logical_not(same(target)))
-        pl.when(meant)(lambda target=target: greet(target))
         greeted += meant.astype(jnp.int32)
     for meant, target in (
         (has_before, before_device), (has_after, after_device), (stencil, (lat, left)), (stencil, (lat, right)),
@@ -256,6 +258,15 @@
     loaded(0)
     pl.when(source)(lambda: gather(0))
     pl.semaphore_wait(barrier, greeted)
+
+    @pl.when(helps)
+    def _():
+        for to_core in range(2):
+            target = member(helped, z, to_core)
+            pl.when(jnp.logical_not(same(target)))(
+                lambda target=target: pl.semaphore_signal(go, inc=1, device_id=target, device_id_type=MESH)
+            )
+
     pl.when(source)(lambda: send_rows(0))
     loaded(1, 2)
 
@@ -276,6 +287,7 @@
         remote(packed.at[0], sides.at[0], send_s.at[0], recv_s.at[0], (lat, right))
         remote(packed.at[1], sides.at[1], send_s.at[1], recv_s.at[1], (lat, left))
 
+    pl.when(helped_from_afar)(lambda: pl.semaphore_wait(go, 1))
     for g in range(2):
         per = 3 * len(GROUPS[g])
         each_size(lambda size, g=g, per=per: landed(relay[g].at[pl.ds(0, size * per)], recv_a.at[g]))
@@ -659,6 +671,7 @@
             pltpu.VMEM((2, ROWS, 128), F32),
             pltpu.VMEM((2, ROWS, 128), F32),
             pltpu.VMEM((3, ROWS + 16, 512), F32),
+            pltpu.SemaphoreType.REGULAR,
             dma((8,)), dma((2, 3)), dma((2,)), dma((2,)), dma((2,)), dma((2,)), dma((2,)), dma((2,)), dma((2, 3)),
             dma((3, 2)), dma((3, 2)), dma((2,)), dma((2,)), dma((2,)), dma((2,)),
         ],

time: 56.4 us -> 55.4 us (0.982)
  the two profiles are of different devices: /device:TPU:1 before, /device:TPU:29 now
where the time goes in v6:
time: 55.4 us; the launch traced here: 55.3 us
  Pallas kernels  54 us (97%)
  between operations  1.29 us (2%)
    pallas_call x1, Pallas kernels, body(): pl.pallas_call(kernel, out_shape=[pltpu.VMEM(block.shape, F32)] * 3, in_s...  53.2 us

profile of v6, /device:TPU:29, one launch (start us, length us, event | category | flops | bytes accessed | tf_op | source)
XLA Modules:
  0.0 55.3 jit_solution(16200145334373458035)
XLA Ops:
  1.3 53.2 %substeps.1 = (f32[1,96,384]{2,1,0:T(8,128)S(1)}, f32[1,96,384]{2,1,0:T(8,128)S(1)}, f32[1,96,384]{2,1,0:T(8,128)S(1)}) custom-call(f32[1]{0:T(128)S(6)} %copy.12.speed_ref, f32[1,96,384]{2,1,0:T(8,128)} %h_hbm.1, f32[1,96,384]{2,1,0:T(8,128)} %u_hbm.1, f32[1,96,384]{2,1,0:T(8,128)} %v_hbm.1, f32[112,288]{1,0:T(8,128)} %constant.10.clone.first_hbm, ...), custom_call_target="tpu_custom_call" | custom-call | tf_op jit(solution)/shard_map/substeps/pallas_call | solution.py:659
  54.5 0.8 %write.1 = (f32[1,96,384]{2,1,0:T(8,128)}, f32[1,96,384]{2,1,0:T(8,128)}, f32[1,96,384]{2,1,0:T(8,128)}) custom-call(f32[1,96,384]{2,1,0:T(8,128)S(1)} %get-tuple-element.6.h_ref, f32[1,96,384]{2,1,0:T(8,128)S(1)} %get-tuple-element.7.u_ref, f32[1,96,384]{2,1,0:T(8,128)S(1)} %get-tuple-element.8.v_ref), custom_call_target="tpu_custom_call" | custom-call | tf_op jit(solution)/shard_map/write/pallas_call | solution.py:683

commit v7 on v6

--- a/solution.py
+++ b/solution.py
@@ -466,14 +466,12 @@
             )
 
         def both(k, carry):
-            to = chip(k)
-            one(remote, to, 0)
-            one(remote, to, 1)
+            to = jnp.where(k < 5, lax.rem(z + k, 5), 5 + lax.rem(z + k, 11))
+            one(send, to, 0)
+            one(send, to, 1)
             return carry
 
-        lax.fori_loop(0, 15, both, 0)
-        one(send, z, 0)
-        one(send, z, 1)
+        lax.fori_loop(0, 16, both, 0)
 
     @pl.when(owner)
     def _():
@@ -520,18 +518,6 @@
         restore(1, last)
         send_back(1)
 
-    for g in range(2):
-        per = 3 * len(BACK[g])
-
-        def deliver(size, g=g, per=per):
-            landed(home[g].at[pl.ds(0, size * per)], recv_c.at[g])
-            send(
-                home[g].at[pl.ds(0, size * per)], ret[g].at[pl.ds(part_start(my_part, size) * per, size * per)],
-                send_d.at[g], recv_d.at[g, my_part], (my_lat, slab),
-            )
-
-        each_size(deliver)
-
     @pl.when(stencil)
     def _():
         @pl.when(lat > 2)
@@ -565,6 +551,18 @@
             height = height - speed * spread_out
         for out, value in zip(outs, (height, east, north)):
             out[0] = value[8 : 8 + ROWS, 0:CELLS]
+
+    for g in range(2):
+        per = 3 * len(BACK[g])
+
+        def deliver(size, g=g, per=per):
+            landed(home[g].at[pl.ds(0, size * per)], recv_c.at[g])
+            send(
+                home[g].at[pl.ds(0, size * per)], ret[g].at[pl.ds(part_start(my_part, size) * per, size * per)],
+                send_d.at[g], recv_d.at[g, my_part], (my_lat, slab),
+            )
+
+        each_size(deliver)
 
     def back(f, s):
         g = 0 if f in BACK[0] else 1

time: 55.4 us -> 54.5 us (0.984)
  the two profiles are of different devices: /device:TPU:29 before, /device:TPU:1 now
where the time goes in v7:
time: 54.5 us; the launch traced here: 53.8 us
  Pallas kernels  52.6 us (97%)
  between operations  1.29 us (2%)
    pallas_call x1, Pallas kernels, body(): pl.pallas_call(kernel, out_shape=[pltpu.VMEM(block.shape, F32)] * 3, in_s...  51.8 us

profile of v7, /device:TPU:1, one launch (start us, length us, event | category | flops | bytes accessed | tf_op | source)
XLA Modules:
  0.0 53.8 jit_solution(14246587624913867629)
XLA Ops:
  1.3 51.8 %substeps.1 = (f32[1,96,384]{2,1,0:T(8,128)S(1)}, f32[1,96,384]{2,1,0:T(8,128)S(1)}, f32[1,96,384]{2,1,0:T(8,128)S(1)}) custom-call(f32[1]{0:T(128)S(6)} %copy.12.speed_ref, f32[1,96,384]{2,1,0:T(8,128)} %h_hbm.1, f32[1,96,384]{2,1,0:T(8,128)} %u_hbm.1, f32[1,96,384]{2,1,0:T(8,128)} %v_hbm.1, f32[112,288]{1,0:T(8,128)} %constant.10.clone.first_hbm, ...), custom_call_target="tpu_custom_call" | custom-call | tf_op jit(solution)/shard_map/substeps/pallas_call | solution.py:657
  53.0 0.8 %write.1 = (f32[1,96,384]{2,1,0:T(8,128)}, f32[1,96,384]{2,1,0:T(8,128)}, f32[1,96,384]{2,1,0:T(8,128)}) custom-call(f32[1,96,384]{2,1,0:T(8,128)S(1)} %get-tuple-element.6.h_ref, f32[1,96,384]{2,1,0:T(8,128)S(1)} %get-tuple-element.7.u_ref, f32[1,96,384]{2,1,0:T(8,128)S(1)} %get-tuple-element.8.v_ref), custom_call_target="tpu_custom_call" | custom-call | tf_op jit(solution)/shard_map/write/pallas_call | solution.py:681

commit v8 on v7

--- a/solution.py
+++ b/solution.py
@@ -101,7 +101,11 @@
     core = lax.rem(band, 2)
     z = lax.rem(lon, 16)
     x = 2 * lax.div(lon, 16) + lax.rem(lax.div(band, 2), 2)
-    line = jnp.where(band < 4, x, 7 - x)
+
+    def back_row(n):
+        return jnp.where(n == 5, 1, jnp.where(n == 6, 2, jnp.where(n == 1, 5, jnp.where(n == 2, 6, 7 - n))))
+
+    line = jnp.where(band < 4, x, back_row(x))
     wide = line >= 6
     near = lax.rem(z + line, 16)
     slab = 16 * core + z
@@ -117,7 +121,7 @@
     my_part = line - 3 * my_band
 
     def member(to_line, to_z, to_core):
-        to_x = jnp.where(to_line < 4, to_line, 7 - to_line)
+        to_x = jnp.where(to_line < 4, to_line, back_row(to_line))
         to_band = 4 * lax.div(to_line, 4) + 2 * lax.rem(to_x, 2) + to_core
         return jnp.where(south, 15 - to_band, to_band), 16 * lax.div(to_x, 2) + to_z
 
@@ -185,28 +189,34 @@
     def greet_other(target):
         pl.when(jnp.logical_not(same(target)))(lambda: greet(target))
 
+    pl.when(jnp.logical_not(same((my_lat, slab))))(lambda: greet((my_lat, slab)))
+
+    def load(*indices):
+        for index in indices:
+            pltpu.make_async_copy(operands[index], held[index], loads.at[index]).start()
+
+    def loaded(*indices):
+        for index in indices:
+            pltpu.make_async_copy(operands[index], held[index], loads.at[index]).wait()
+
+    load(0, 1, 2)
+    pl.when(owner)(lambda: load(3, 4, 5, 6, 7))
+
     def helper(of_line, to_z):
-        of_x = jnp.where(of_line < 4, of_line, 7 - of_line)
-        return member(7 - of_x, to_z, lax.div(of_line, 4))
+        of_x = jnp.where(of_line < 4, of_line, back_row(of_line))
+        return member(back_row(of_x), to_z, lax.div(of_line, 4))
 
     helps = band >= 4
-    helped = jnp.where(core == 1, 7 - x, x)
+    helped = jnp.where(core == 1, back_row(x), x)
 
     def greet_helper(k, carry):
-        greet(helper(line, lax.rem(z + k, 16)))
+        greet(helper(line, chip(k)))
         return carry
 
     my_helper = helper(line, z)
     helped_from_afar = jnp.logical_not(same(my_helper))
 
-    @pl.when(owner)
-    def _():
-        lax.fori_loop(1, 16, greet_helper, 0)
-
-    pl.when(jnp.logical_and(owner, helped_from_afar))(lambda: greet(my_helper))
-    pl.when(helped_from_afar)(lambda: greet(my_helper))
     greeted = jnp.where(helps, jnp.where(helped >= 6, 18, 16) + 2 - 2 * core, 0)
-    pl.when(jnp.logical_not(same((my_lat, slab))))(lambda: greet((my_lat, slab)))
     for k in range(3):
         target = member(jnp.minimum(3 * band + k, 7), z, lax.div(lon, 16))
         meant = jnp.logical_or(band < 2, jnp.logical_and(band == 2, k < 2))
@@ -219,16 +229,12 @@
         pl.when(meant)(lambda target=target: greet(target))
         greeted += meant.astype(jnp.int32)
 
-    def load(*indices):
-        for index in indices:
-            pltpu.make_async_copy(operands[index], held[index], loads.at[index]).start()
-
-    def loaded(*indices):
-        for index in indices:
-            pltpu.make_async_copy(operands[index], held[index], loads.at[index]).wait()
-
-    load(0, 1, 2)
-    pl.when(owner)(lambda: load(3, 4, 5, 6, 7))
+    @pl.when(owner)
+    def _():
+        lax.fori_loop(0, 15, greet_helper, 0)
+
+    pl.when(jnp.logical_and(owner, helped_from_afar))(lambda: greet(my_helper))
+    pl.when(helped_from_afar)(lambda: greet(my_helper))
 
     def gather(g):
         per = 3 * len(GROUPS[g])

time: 54.5 us -> 55.1 us (1.011)
  the two profiles are of different devices: /device:TPU:1 before, /device:TPU:25 now
where the time goes in v8:
time: 55.1 us; the launch traced here: 54.9 us
  Pallas kernels  53.6 us (97%)
  between operations  1.29 us (2%)
    pallas_call x1, Pallas kernels, body(): pl.pallas_call(kernel, out_shape=[pltpu.VMEM(block.shape, F32)] * 3, in_s...  52.8 us

profile of v8, /device:TPU:25, one launch (start us, length us, event | category | flops | bytes accessed | tf_op | source)
XLA Modules:
  0.0 54.9 jit_solution(8142728353042402026)
XLA Ops:
  1.3 52.8 %substeps.1 = (f32[1,96,384]{2,1,0:T(8,128)S(1)}, f32[1,96,384]{2,1,0:T(8,128)S(1)}, f32[1,96,384]{2,1,0:T(8,128)S(1)}) custom-call(f32[1]{0:T(128)S(6)} %copy.12.speed_ref, f32[1,96,384]{2,1,0:T(8,128)} %h_hbm.1, f32[1,96,384]{2,1,0:T(8,128)} %u_hbm.1, f32[1,96,384]{2,1,0:T(8,128)} %v_hbm.1, f32[112,288]{1,0:T(8,128)} %constant.10.clone.first_hbm, ...), custom_call_target="tpu_custom_call" | custom-call | tf_op jit(solution)/shard_map/substeps/pallas_call | solution.py:663
  54.1 0.8 %write.1 = (f32[1,96,384]{2,1,0:T(8,128)}, f32[1,96,384]{2,1,0:T(8,128)}, f32[1,96,384]{2,1,0:T(8,128)}) custom-call(f32[1,96,384]{2,1,0:T(8,128)S(1)} %get-tuple-element.6.h_ref, f32[1,96,384]{2,1,0:T(8,128)S(1)} %get-tuple-element.7.u_ref, f32[1,96,384]{2,1,0:T(8,128)S(1)} %get-tuple-element.8.v_ref), custom_call_target="tpu_custom_call" | custom-call | tf_op jit(solution)/shard_map/write/pallas_call | solution.py:687

commit v9 on v8

--- a/solution.py
+++ b/solution.py
@@ -22,6 +22,7 @@
 MESH = pl.DeviceIdType.MESH
 F32, BF16 = jnp.float32, jnp.bfloat16
 GROUPS = ((0,), (1, 2))
+BACK_ROW = (3, 2, 1, 0)
 BACK = ((1,), (2, 0))
 
 
@@ -102,17 +103,24 @@
     z = lax.rem(lon, 16)
     x = 2 * lax.div(lon, 16) + lax.rem(lax.div(band, 2), 2)
 
-    def back_row(n):
-        return jnp.where(n == 5, 1, jnp.where(n == 6, 2, jnp.where(n == 1, 5, jnp.where(n == 2, 6, 7 - n))))
-
-    line = jnp.where(band < 4, x, back_row(x))
+    def back_x(n):
+        return jnp.where(n == 4, BACK_ROW[0], jnp.where(n == 5, BACK_ROW[1], jnp.where(n == 6, BACK_ROW[2], BACK_ROW[3])))
+
+    def back_line(n):
+        return jnp.where(n == BACK_ROW[0], 4, jnp.where(n == BACK_ROW[1], 5, jnp.where(n == BACK_ROW[2], 6, 7)))
+
+    line = jnp.where(band < 4, x, back_line(x))
     wide = line >= 6
     near = lax.rem(z + line, 16)
     slab = 16 * core + z
-    extra = jnp.logical_and(wide, jnp.logical_and(core == 0, jnp.logical_or(near == 0, near == 15)))
+    extra = jnp.logical_and(wide, jnp.logical_and(core == 0, jnp.logical_or(near == 0, near == 8)))
     owner = jnp.logical_or(core == 1, extra)
     owners = jnp.where(wide, 18, 16)
-    nth = jnp.where(wide, jnp.where(core == 1, near + 1, jnp.where(near == 0, 0, 17)), near)
+
+    def nth_at(to_near):
+        return to_near + jnp.where(wide, 1 + jnp.where(to_near > 8, 1, 0), 0)
+
+    nth = jnp.where(core == 1, nth_at(near), jnp.where(near == 0, 0, 10))
     chain = 16 * line + 2 * jnp.where(line == 7, 1, 0) + nth
     source = band <= 2
     stencil = band >= 2
@@ -121,7 +129,7 @@
     my_part = line - 3 * my_band
 
     def member(to_line, to_z, to_core):
-        to_x = jnp.where(to_line < 4, to_line, back_row(to_line))
+        to_x = jnp.where(to_line < 4, to_line, back_x(to_line))
         to_band = 4 * lax.div(to_line, 4) + 2 * lax.rem(to_x, 2) + to_core
         return jnp.where(south, 15 - to_band, to_band), 16 * lax.div(to_x, 2) + to_z
 
@@ -133,8 +141,8 @@
         to_line = jnp.where(n < 96, lax.div(n, 16), 6 + lax.div(jnp.maximum(n - 96, 0), 18))
         to_nth = n - 16 * to_line - 2 * jnp.where(to_line == 7, 1, 0)
         broad = to_line >= 6
-        to_near = jnp.where(broad, jnp.clip(to_nth - 1, 0, 15), to_nth)
-        to_core = jnp.where(jnp.logical_and(broad, jnp.logical_or(to_nth == 0, to_nth == 17)), 0, 1)
+        to_near = jnp.where(broad, jnp.maximum(to_nth - jnp.where(to_nth > 9, 2, 1), 0), to_nth)
+        to_core = jnp.where(jnp.logical_and(broad, jnp.logical_or(to_nth == 0, to_nth == 10)), 0, 1)
         return member(to_line, lax.rem(to_near + 16 - to_line, 16), to_core)
 
     def chip(k):
@@ -203,11 +211,11 @@
     pl.when(owner)(lambda: load(3, 4, 5, 6, 7))
 
     def helper(of_line, to_z):
-        of_x = jnp.where(of_line < 4, of_line, back_row(of_line))
-        return member(back_row(of_x), to_z, lax.div(of_line, 4))
+        of_x = jnp.where(of_line < 4, of_line, back_x(of_line))
+        return member(back_line(of_x), to_z, lax.div(of_line, 4))
 
     helps = band >= 4
-    helped = jnp.where(core == 1, back_row(x), x)
+    helped = jnp.where(core == 1, back_line(x), x)
 
     def greet_helper(k, carry):
         greet(helper(line, chip(k)))
@@ -307,16 +315,16 @@
 
         def spread(k, carry, to_owner=to_owner):
             to = chip(k)
-            to_owner(remote, lax.rem(to + line, 16) + jnp.where(wide, 1, 0), mate(to, 1))
+            to_owner(remote, nth_at(lax.rem(to + line, 16)), mate(to, 1))
             return carry
 
         @pl.when(wide)
         def _(to_owner=to_owner):
-            for i in (0, 17):
-                to_owner(send, i, mate(lax.rem(min(i, 15) + 16 - line, 16), 0))
+            for i, to_near in ((0, 0), (10, 8)):
+                to_owner(send, i, mate(lax.rem(to_near + 16 - line, 16), 0))
 
         lax.fori_loop(0, 15, spread, 0)
-        to_owner(send, near + jnp.where(wide, 1, 0), mate(z, 1))
+        to_owner(send, nth_at(near), mate(z, 1))
 
     @pl.when(stencil)
     def _():

time: 55.1 us -> 53.4 us (0.969)
  the two profiles are of different devices: /device:TPU:25 before, /device:TPU:1 now
where the time goes in v9:
time: 53.4 us; the launch traced here: 52.9 us
  Pallas kernels  51.7 us (97%)
  between operations  1.29 us (2%)
    pallas_call x1, Pallas kernels, body(): pl.pallas_call(kernel, out_shape=[pltpu.VMEM(block.shape, F32)] * 3, in_s...  50.9 us

profile of v9, /device:TPU:1, one launch (start us, length us, event | category | flops | bytes accessed | tf_op | source)
XLA Modules:
  0.0 52.9 jit_solution(9429306733262549205)
XLA Ops:
  1.3 50.9 %substeps.1 = (f32[1,96,384]{2,1,0:T(8,128)S(1)}, f32[1,96,384]{2,1,0:T(8,128)S(1)}, f32[1,96,384]{2,1,0:T(8,128)S(1)}) custom-call(f32[1]{0:T(128)S(6)} %copy.12.speed_ref, f32[1,96,384]{2,1,0:T(8,128)} %h_hbm.1, f32[1,96,384]{2,1,0:T(8,128)} %u_hbm.1, f32[1,96,384]{2,1,0:T(8,128)} %v_hbm.1, f32[112,288]{1,0:T(8,128)} %constant.10.clone.first_hbm, ...), custom_call_target="tpu_custom_call" | custom-call | tf_op jit(solution)/shard_map/substeps/pallas_call | solution.py:671
  52.2 0.8 %write.1 = (f32[1,96,384]{2,1,0:T(8,128)}, f32[1,96,384]{2,1,0:T(8,128)}, f32[1,96,384]{2,1,0:T(8,128)}) custom-call(f32[1,96,384]{2,1,0:T(8,128)S(1)} %get-tuple-element.6.h_ref, f32[1,96,384]{2,1,0:T(8,128)S(1)} %get-tuple-element.7.u_ref, f32[1,96,384]{2,1,0:T(8,128)S(1)} %get-tuple-element.8.v_ref), custom_call_target="tpu_custom_call" | custom-call | tf_op jit(solution)/shard_map/write/pallas_call | solution.py:695

commit v10 on v9

--- a/solution.py
+++ b/solution.py
@@ -476,7 +476,7 @@
         def one(how, to_z, to_core):
             how(
                 snd[g].at[pl.ds((16 * to_core + to_z) * size, size)], home[g].at[pl.ds(start, size)],
-                send_c.at[g], recv_c.at[g], mate(to_z, to_core),
+                send_c.at[g], recv_c.at[g, lax.div(near, 4) if g else 0], mate(to_z, to_core),
             )
 
         def both(k, carry):
@@ -566,17 +566,37 @@
         for out, value in zip(outs, (height, east, north)):
             out[0] = value[8 : 8 + ROWS, 0:CELLS]
 
-    for g in range(2):
-        per = 3 * len(BACK[g])
-
-        def deliver(size, g=g, per=per):
-            landed(home[g].at[pl.ds(0, size * per)], recv_c.at[g])
+    def deliver(size):
+        per = 3 * len(BACK[0])
+        landed(home[0].at[pl.ds(0, size * per)], recv_c.at[0, 0])
+        send(
+            home[0].at[pl.ds(0, size * per)], ret[0].at[pl.ds(part_start(my_part, size) * per, size * per)],
+            send_d.at[0], recv_d.at[0, my_part], (my_lat, slab),
+        )
+
+    def deliver_quarter(k):
+        per = 3 * len(BACK[1])
+        turn = jnp.where(lax.rem(near, 4) < 2, 3, 1)
+        quarter = lax.rem(lax.div(near, 4) + (0, turn, 4 - turn, 2)[k], 4)
+
+        def rows(size, line_size):
+            first = jnp.where(quarter == 0, 0, nth_at(4 * quarter))
+            start = jnp.where(south, line_size - size - HOLD * first, HOLD * first)
+            here = home[1].at[pl.ds(start * per, size * per)]
+            landed(here, recv_c.at[1, quarter])
             send(
-                home[g].at[pl.ds(0, size * per)], ret[g].at[pl.ds(part_start(my_part, size) * per, size * per)],
-                send_d.at[g], recv_d.at[g, my_part], (my_lat, slab),
+                here, ret[1].at[pl.ds((part_start(my_part, line_size) + start) * per, size * per)],
+                send_d.at[1], recv_d.at[1, my_part], (my_lat, slab),
             )
 
-        each_size(deliver)
+        large = jnp.logical_and(wide, lax.rem(quarter, 2) == 0)
+        pl.when(jnp.logical_not(wide))(lambda: rows(8, 32))
+        pl.when(large)(lambda: rows(10, 36))
+        pl.when(jnp.logical_and(wide, jnp.logical_not(large)))(lambda: rows(8, 36))
+
+    each_size(deliver)
+    for k in range(4):
+        deliver_quarter(k)
 
     def back(f, s):
         g = 0 if f in BACK[0] else 1
@@ -684,7 +704,7 @@
             pltpu.VMEM((2, ROWS, 128), F32),
             pltpu.VMEM((3, ROWS + 16, 512), F32),
             pltpu.SemaphoreType.REGULAR,
-            dma((8,)), dma((2, 3)), dma((2,)), dma((2,)), dma((2,)), dma((2,)), dma((2,)), dma((2,)), dma((2, 3)),
+            dma((8,)), dma((2, 3)), dma((2,)), dma((2,)), dma((2,)), dma((2,)), dma((2, 4)), dma((2,)), dma((2, 3)),
             dma((3, 2)), dma((3, 2)), dma((2,)), dma((2,)), dma((2,)), dma((2,)),
         ],
         compiler_params=pltpu.CompilerParams(

time: 53.4 us -> 52.4 us (0.981)
  Pallas kernels: 51.7 us -> 50.9 us
    pallas_call x1, Pallas kernels: 50.9 us -> 50.1 us  [body(): pl.pallas_call(kernel, out_shape=[pltpu.VMEM(block.shape, F32)] * 3, in_s...]
where the time goes in v10:
time: 52.4 us; the launch traced here: 52.2 us
  Pallas kernels  50.9 us (97%)
  between operations  1.29 us (2%)
    pallas_call x1, Pallas kernels, body(): pl.pallas_call(kernel, out_shape=[pltpu.VMEM(block.shape, F32)] * 3, in_s...  50.1 us

profile of v10, /device:TPU:1, one launch (start us, length us, event | category | flops | bytes accessed | tf_op | source)
XLA Modules:
  0.0 52.2 jit_solution(9103690986221415447)
XLA Ops:
  1.3 50.1 %substeps.1 = (f32[1,96,384]{2,1,0:T(8,128)S(1)}, f32[1,96,384]{2,1,0:T(8,128)S(1)}, f32[1,96,384]{2,1,0:T(8,128)S(1)}) custom-call(f32[1]{0:T(128)S(6)} %copy.12.speed_ref, f32[1,96,384]{2,1,0:T(8,128)} %h_hbm.1, f32[1,96,384]{2,1,0:T(8,128)} %u_hbm.1, f32[1,96,384]{2,1,0:T(8,128)} %v_hbm.1, f32[112,288]{1,0:T(8,128)} %constant.10.clone.first_hbm, ...), custom_call_target="tpu_custom_call" | custom-call | tf_op jit(solution)/shard_map/substeps/pallas_call | solution.py:691
  51.4 0.8 %write.1 = (f32[1,96,384]{2,1,0:T(8,128)}, f32[1,96,384]{2,1,0:T(8,128)}, f32[1,96,384]{2,1,0:T(8,128)}) custom-call(f32[1,96,384]{2,1,0:T(8,128)S(1)} %get-tuple-element.6.h_ref, f32[1,96,384]{2,1,0:T(8,128)S(1)} %get-tuple-element.7.u_ref, f32[1,96,384]{2,1,0:T(8,128)S(1)} %get-tuple-element.8.v_ref), custom_call_target="tpu_custom_call" | custom-call | tf_op jit(solution)/shard_map/write/pallas_call | solution.py:715

commit v11 on v10

--- a/solution.py
+++ b/solution.py
@@ -480,9 +480,9 @@
             )
 
         def both(k, carry):
-            to = jnp.where(k < 5, lax.rem(z + k, 5), 5 + lax.rem(z + k, 11))
-            one(send, to, 0)
-            one(send, to, 1)
+            to = jnp.where(k < 1, 0 + lax.rem(z + k, 1), jnp.where(k < 3, 1 + lax.rem(z + k, 2), jnp.where(k < 6, 3 + lax.rem(z + k, 3), 6 + lax.rem(z + k, 10))))
+            one(remote, to, 1 - core)
+            one(send, to, core)
             return carry
 
         lax.fori_loop(0, 16, both, 0)

time: 52.4 us -> 52.1 us (level)
  no operation moved by 1% of the time
where the time goes in v11:
time: 52.1 us; the launch traced here: 51.9 us
  Pallas kernels  50.6 us (97%)
  between operations  1.29 us (2%)
    pallas_call x1, Pallas kernels, body(): pl.pallas_call(kernel, out_shape=[pltpu.VMEM(block.shape, F32)] * 3, in_s...  49.9 us

profile of v11, /device:TPU:1, one launch (start us, length us, event | category | flops | bytes accessed | tf_op | source)
XLA Modules:
  0.0 51.9 jit_solution(12898118989657462018)
XLA Ops:
  1.3 49.9 %substeps.1 = (f32[1,96,384]{2,1,0:T(8,128)S(1)}, f32[1,96,384]{2,1,0:T(8,128)S(1)}, f32[1,96,384]{2,1,0:T(8,128)S(1)}) custom-call(f32[1]{0:T(128)S(6)} %copy.12.speed_ref, f32[1,96,384]{2,1,0:T(8,128)} %h_hbm.1, f32[1,96,384]{2,1,0:T(8,128)} %u_hbm.1, f32[1,96,384]{2,1,0:T(8,128)} %v_hbm.1, f32[112,288]{1,0:T(8,128)} %constant.10.clone.first_hbm, ...), custom_call_target="tpu_custom_call" | custom-call | tf_op jit(solution)/shard_map/substeps/pallas_call | solution.py:691
  51.1 0.8 %write.1 = (f32[1,96,384]{2,1,0:T(8,128)}, f32[1,96,384]{2,1,0:T(8,128)}, f32[1,96,384]{2,1,0:T(8,128)}) custom-call(f32[1,96,384]{2,1,0:T(8,128)S(1)} %get-tuple-element.6.h_ref, f32[1,96,384]{2,1,0:T(8,128)S(1)} %get-tuple-element.7.u_ref, f32[1,96,384]{2,1,0:T(8,128)S(1)} %get-tuple-element.8.v_ref), custom_call_target="tpu_custom_call" | custom-call | tf_op jit(solution)/shard_map/write/pallas_call | solution.py:715
